TPU v7x, 128 devices: a whole 4x4x4 slice. The times are simulated.
128 devices in a mesh: dp: 2 (over core), ctx: 16 (over y, x), head: 4 (over z).
Axes of the slice: x: 4, y: 4, z: 4, core: 2. Of those that a mesh axis runs over, the one named last changes fastest.
Arguments:
- xbc_raw: bfloat16 [2, 8192, 10240], P('dp', ('ctx', 'head')), may hold values from -6 to 6
- gate_raw: bfloat16 [2, 8192, 8192], P('dp', ('ctx', 'head')), may hold values from -6 to 6
- dt_raw: bfloat16 [2, 8192, 128], P('dp', ('ctx', 'head')), may hold values from -3 to 63
- segment_ids: int32 [2, 8192], P('dp', ('ctx', 'head')), may hold values from 0 to 3, never falling along the last dimension, each value on 1 to 4096 neighbouring positions
- conv_weight: float32 [5, 10240], P(None, 'head'), may hold values from -3 to 3
- norm_gain: float32 [8192], P('head'), may hold values from 0.5 to 1.5
- head_params: float32 [3, 128], P(None, 'head'), may hold values from -11 to 1.5
- out_cotangent: bfloat16 [2, 8192, 8192], P('dp', ('ctx', 'head')), may hold values from -6 to 6
Outputs:
- grad_xbc: bfloat16 [2, 8192, 10240], P('dp', ('ctx', 'head'))
- grad_gate: bfloat16 [2, 8192, 8192], P('dp', ('ctx', 'head'))
- grad_dt: bfloat16 [2, 8192, 128], P('dp', ('ctx', 'head'))
- grad_conv: float32 [5, 10240], P(None, 'head')
- grad_gain: float32 [8192], P('head')
- grad_heads: float32 [3, 128], P(None, 'head')
Inputs may be any that keep to these rules, and one draw needn't show every extreme that they name: `segment_ids`: segment ids never fall along a sequence; every document holds at most 4096 positions and one holds exactly that many.
All inputs are finite; a program needn't handle non-finite values.
Results may differ from a plain program's by a relative error of at most 0.025.
The roundings to bfloat16 on the way count: a program that leaves them out, or rounds other values in their place, can miss the bound.
Values may be sent and summed in bfloat16 or wider, within the bound.
A program may use at most 256 MiB of HBM per device.

v0:
```python
from functools import partial

import jax
import jax.numpy as jnp
from jax import lax
from jax.sharding import PartitionSpec as P

OWNED_MIXERS = 128
HEAD_DIM = 64
STATE = 128
GROUPS = 8


highest = lax.Precision.HIGHEST
triple = lax.Precision.HIGH


def shifted(value, axis, steps):
    count = lax.axis_size(axis)
    leading, last = (max(0, -steps), min(count, count - steps))
    return lax.ppermute(value, axis, [(source, source + steps) for source in range(leading, last)])


def prefix(part, axis, combine, identity, reverse):
    count = lax.axis_size(axis)
    place = lax.axis_index(axis)
    ahead = count - 1 - place if reverse else place
    gathered = jax.tree.map(lambda a: lax.all_gather(a, axis), part)
    state = jax.tree.map(lambda a, e: jnp.zeros_like(a) + jnp.asarray(e, a.dtype), part, identity)

    def one(hop, state):
        source = count - 1 - hop if reverse else hop
        return combine(
            state, jax.tree.map(lambda a: lax.dynamic_index_in_dim(a, source, 0, False), gathered)
        )

    return lax.fori_loop(0, ahead, one, state)


def conv_block(extended, conv_taps, segment_ext, conv_width):
    row_count = extended.shape[0] - conv_width + 1
    segment_now = segment_ext[conv_width - 1 :]
    summed = jnp.broadcast_to(conv_taps[conv_width], (row_count, conv_taps.shape[1]))
    for tap_index in range(conv_width):
        window = extended[tap_index : tap_index + row_count]
        same_doc = (segment_ext[tap_index : tap_index + row_count] == segment_now).astype(
            extended.dtype
        )
        summed = summed + conv_taps[tap_index] * window * same_doc[:, None]
    return summed


def split_channels(act_values, group_count):
    row_count = act_values.shape[0]
    grouped = act_values.reshape(row_count, group_count, -1)
    x_width = grouped.shape[2] - 2 * STATE
    per_group = x_width // HEAD_DIM
    x_part = grouped[:, :, :x_width].reshape(row_count, group_count, per_group, HEAD_DIM)
    b_part = grouped[:, :, x_width : x_width + STATE]
    c_part = grouped[:, :, x_width + STATE :]
    return (x_part, b_part, c_part)


def span_step(state_now, inputs):
    x_part, b_part, c_part, step_size, log_decay, seg_span, seg_prev = inputs
    span_len = seg_span.shape[0]
    running = jnp.cumsum(log_decay, axis=0)
    positions = jnp.arange(span_len)
    inside = (seg_span[:, None] == seg_span[None, :]) & (positions[:, None] >= positions[None, :])
    run_moved = jnp.transpose(running, (1, 2, 0))
    gap_values = run_moved[:, :, :, None] - run_moved[:, :, None, :]
    decay_mat = jnp.where(inside, jnp.exp(jnp.where(inside, gap_values, 0.0)), 0.0)
    scores = jnp.einsum("tgn,sgn->gts", c_part, b_part, precision=triple)
    step_moved = jnp.transpose(step_size, (1, 2, 0))
    weights = decay_mat * scores[:, None] * step_moved[:, :, None, :]
    y_part = jnp.einsum("gjts,sgjp->tgjp", weights, x_part, precision=triple)
    linked = (seg_span == seg_prev).astype(running.dtype)
    alive_mask = jnp.exp(running) * linked[:, None, None]
    y_part = y_part + alive_mask[..., None] * jnp.einsum(
        "tgn,gjnp->tgjp", c_part, state_now, precision=highest
    )
    same_last = (seg_span == seg_span[-1]).astype(running.dtype)
    tail_weight = jnp.exp(running[-1][None] - running) * same_last[:, None, None] * step_size
    keep_all = jnp.exp(running[-1]) * linked[-1]
    new_state = keep_all[..., None, None] * state_now + jnp.einsum(
        "sgn,sgj,sgjp->gjnp", b_part, tail_weight, x_part, precision=triple
    )
    return (new_state, y_part)


def scanned_spans(x_part, b_part, c_part, step_size, log_decay, seg_values, seg_before):
    row_count = x_part.shape[0]
    span_len = min(128, row_count)
    span_count = row_count // span_len
    prev_all = jnp.concatenate([jnp.reshape(seg_before, (1,)), seg_values[:-1]])
    span_prev = prev_all.reshape(span_count, span_len)[:, 0]

    def split_up(values_in):
        return values_in.reshape((span_count, span_len) + values_in.shape[1:])

    start_state = jnp.zeros((x_part.shape[1], x_part.shape[2], STATE, HEAD_DIM), x_part.dtype)
    final_state, outputs = lax.scan(
        jax.checkpoint(span_step),
        start_state,
        (
            split_up(x_part),
            split_up(b_part),
            split_up(c_part),
            split_up(step_size),
            split_up(log_decay),
            split_up(seg_values),
            span_prev,
        ),
    )
    return (outputs.reshape(x_part.shape), final_state)


def gate_norm(ssm_values, gate_values, gain_values, group_count):
    gated = ssm_values.astype(jnp.float32) * jax.nn.silu(gate_values.astype(jnp.float32))
    row_count = gated.shape[0]
    grouped = gated.reshape(row_count, group_count, -1)
    mean_sq = jnp.mean(grouped * grouped, axis=-1, keepdims=True)
    return (grouped * lax.rsqrt(mean_sq + 1e-05)).reshape(row_count, -1) * gain_values


def local_block(ext_in, dt_in, conv_in, heads_in, seg_ext, seg_before, group_count, conv_width):
    activated = jax.nn.silu(conv_block(ext_in, conv_in, seg_ext, conv_width))
    activated = lax.optimization_barrier(activated.astype(jnp.bfloat16)).astype(jnp.float32)
    x_part, b_part, c_part = split_channels(activated, group_count)
    row_count = x_part.shape[0]
    per_group = x_part.shape[2]
    step_size = jax.nn.softplus(dt_in + heads_in[1])
    log_decay = -step_size * jnp.exp(heads_in[0])
    shape_three = (row_count, group_count, per_group)
    seg_values = seg_ext[conv_width - 1 :]
    y_zero, block_state = scanned_spans(
        x_part,
        b_part,
        c_part,
        step_size.reshape(shape_three),
        log_decay.reshape(shape_three),
        seg_values,
        seg_before,
    )
    y_zero = y_zero + heads_in[2].reshape(group_count, per_group)[None, :, :, None] * x_part
    running = jnp.cumsum(log_decay.reshape(shape_three), axis=0)
    linked = (seg_values == seg_before).astype(jnp.float32)
    alive_mask = jnp.exp(running) * linked[:, None, None]
    block_decay = jnp.exp(running[-1]) * linked[-1]
    return (y_zero.reshape(row_count, -1), c_part, alive_mask, block_decay, block_state)


def add_carried(y_zero, c_matrix, alive_mask, start_state):
    carried = (
        jnp.einsum("tgn,gjnp->tgjp", c_matrix, start_state, precision=highest)
        * alive_mask[..., None]
    )
    return y_zero + carried.reshape(y_zero.shape)


def compose(earlier, later):
    decay_one, state_one = earlier
    decay_two, state_two = later
    return (decay_two * decay_one, decay_two[..., None, None] * state_one + state_two)


def body(
    xbc_raw, gate_raw, dt_raw, segment_ids, conv_weight, norm_gain, head_params, out_cotangent
):
    xbc_tok = xbc_raw[0]
    gate_tok = gate_raw[0]
    dt_tok = dt_raw[0]
    cot_tok = out_cotangent[0]
    conv_width = conv_weight.shape[0] - 1
    local_heads = head_params.shape[1]
    per_group = OWNED_MIXERS // GROUPS
    local_groups = local_heads // per_group
    seg_block = lax.all_gather(segment_ids, "head", axis=1, tiled=True)[0]
    shifted_ids = shifted(seg_block[seg_block.shape[0] - conv_width + 1 :] + 1, "ctx", 1)
    seg_ext = jnp.concatenate([shifted_ids - 1, seg_block])
    xbc_blk, gate_blk, dt_blk, cot_blk = (
        lax.all_to_all(xbc_tok, "head", split_axis=1, concat_axis=0, tiled=True),
        lax.all_to_all(gate_tok, "head", split_axis=1, concat_axis=0, tiled=True),
        lax.all_to_all(dt_tok, "head", split_axis=1, concat_axis=0, tiled=True),
        lax.all_to_all(cot_tok, "head", split_axis=1, concat_axis=0, tiled=True),
    )
    block_rows = xbc_blk.shape[0]
    seg_before = seg_ext[conv_width - 2]
    rim_rows = shifted(xbc_blk[block_rows - conv_width + 1 :], "ctx", 1)
    extended = jnp.concatenate([rim_rows, xbc_blk]).astype(jnp.float32)
    dt_values = dt_blk.astype(jnp.float32)

    def local_part(ext_in, dt_in, conv_in, heads_in):
        return local_block(
            ext_in, dt_in, conv_in, heads_in, seg_ext, seg_before, local_groups, conv_width
        )

    (y_zero, c_matrix, alive_mask, block_decay, block_state), pull_local = jax.vjp(
        local_part, extended, dt_values, conv_weight, head_params
    )
    identity = (jnp.ones_like(block_decay), jnp.zeros_like(block_state))
    start_state = prefix((block_decay, block_state), "ctx", compose, identity, False)[1]
    ssm_f32, pull_state = jax.vjp(add_carried, y_zero, c_matrix, alive_mask, start_state)
    ssm_bf = lax.optimization_barrier(ssm_f32.astype(jnp.bfloat16))
    out_values, pull_gate = jax.vjp(
        partial(gate_norm, group_count=local_groups), ssm_bf, gate_blk, norm_gain
    )
    grad_ssm, grad_gate_blk, grad_gain = pull_gate(cot_blk.astype(jnp.float32))
    grad_y_zero, grad_c, grad_alive, carried_grad = pull_state(grad_ssm.astype(jnp.float32))
    end_grad = prefix((block_decay, carried_grad), "ctx", compose, identity, True)[1]
    decay_grad = jnp.sum(end_grad * start_state, axis=(2, 3))
    grad_ext, grad_dt_blk, grad_conv, grad_heads = pull_local(
        (grad_y_zero, grad_c, grad_alive, decay_grad, end_grad)
    )
    rim_grad = shifted(grad_ext[: conv_width - 1], "ctx", -1)
    grad_rows = grad_ext[conv_width - 1 :]
    grad_rows = grad_rows.at[block_rows - conv_width + 1 :].add(rim_grad)
    grad_xbc_blk = grad_rows.astype(jnp.bfloat16)
    grad_dt_bf = grad_dt_blk.astype(jnp.bfloat16)
    grad_xbc_tok, grad_gate_tok, grad_dt_tok = (
        lax.all_to_all(grad_xbc_blk, "head", split_axis=0, concat_axis=1, tiled=True),
        lax.all_to_all(grad_gate_blk, "head", split_axis=0, concat_axis=1, tiled=True),
        lax.all_to_all(grad_dt_bf, "head", split_axis=0, concat_axis=1, tiled=True),
    )
    grad_conv, grad_gain, grad_heads = (
        lax.psum(grad_conv.astype(jnp.bfloat16), ("dp", "ctx")).astype(jnp.float32),
        lax.psum(grad_gain.astype(jnp.bfloat16), ("dp", "ctx")).astype(jnp.float32),
        lax.psum(grad_heads.astype(jnp.bfloat16), ("dp", "ctx")).astype(jnp.float32),
    )
    return (
        grad_xbc_tok[None],
        grad_gate_tok[None],
        grad_dt_tok[None],
        grad_conv,
        grad_gain,
        grad_heads,
    )


def solution(mesh):
    return jax.shard_map(
        body,
        mesh=mesh,
        in_specs=(
            P("dp", ("ctx", "head"), None),
            P("dp", ("ctx", "head"), None),
            P("dp", ("ctx", "head"), None),
            P("dp", ("ctx", "head")),
            P(None, "head"),
            P("head"),
            P(None, "head"),
            P("dp", ("ctx", "head"), None),
        ),
        out_specs=(
            P("dp", ("ctx", "head"), None),
            P("dp", ("ctx", "head"), None),
            P("dp", ("ctx", "head"), None),
            P(None, "head"),
            P("head"),
            P(None, "head"),
        ),
        check_vma=False,
    )
```

profile of v0, /device:TPU:1, one launch (start us, length us, event | category | flops | bytes accessed | tf_op | source)
XLA Modules:
  0.0 1288.4 jit_solution(14919439984861785439)
XLA Ops:
  17.5 32.9 %all_gather.21 = s32[1,512]{1,0:T(1,128)} all-gather(s32[1,128]{1,0:T(1,128)S(1)} %copy-done.70), channel_id=1, replica_groups=mesh['dp'=2,'ctx'=16,'head'=4] {'head'}, dimensions={1}, use_global_device_ids=true | all-gather | bytes 2560 | tf_op jit(solution)/shard_map/all_gather | solution.py:178
  77.6 8.1 multiply_convert_fusion
  103.9 185.1 %while.71 = (s32[]{:T(128)}, f32[2,16,128,64]{2,3,1,0:T(8,128)S(1)}, f32[4,128,2,16,64]{1,0,4,3,2:T(4,128)}, f32[4,2,16,128,64]{3,4,2,1,0:T(8,128)}, f32[4,128,2...) while((s32[]{:T(128)}, ...), condition=%wide.region_2.3_spmd.clone, body=%wide.region_0.2_spmd.clone.sunk | while | flops 835252736 | bytes 14953431 | solution.py:102
  120.1 26.4 %dynamic_update_slice.79 = f32[4,128,2,16,64]{1,0,4,3,2:T(4,128)} dynamic-update-slice(f32[4,128,2,16,64]{1,0,4,3,2:T(4,128)} %get-tuple-element.1492, f32[1,128,2,16,64]{1,0,4,3,2:T(1,128)S(1)} %bitcast.617, s32[]{:T(128)} %get-tuple-element.1490, s32[]{:T(128)} %constant.207.clone.1..sunk.3, s32[]{:T(128)} %constant.207.clone.1..sunk.3, s32[]{:T(128)} %constant.207.clone.1..sunk.3, ...) | dynamic-update-slice | bytes 2097156 | tf_op jit(solution)/shard_map/jvp()/while/body/jit(dynamic_update_index_in_dim)/dynamic_update_slice | solution.py:102
  166.3 26.4 %dynamic_update_slice.79 = f32[4,128,2,16,64]{1,0,4,3,2:T(4,128)} dynamic-update-slice(f32[4,128,2,16,64]{1,0,4,3,2:T(4,128)} %get-tuple-element.1492, f32[1,128,2,16,64]{1,0,4,3,2:T(1,128)S(1)} %bitcast.617, s32[]{:T(128)} %get-tuple-element.1490, s32[]{:T(128)} %constant.207.clone.1..sunk.3, s32[]{:T(128)} %constant.207.clone.1..sunk.3, s32[]{:T(128)} %constant.207.clone.1..sunk.3, ...) | dynamic-update-slice | bytes 2097156 | tf_op jit(solution)/shard_map/jvp()/while/body/jit(dynamic_update_index_in_dim)/dynamic_update_slice | solution.py:102
  212.6 26.4 %dynamic_update_slice.79 = f32[4,128,2,16,64]{1,0,4,3,2:T(4,128)} dynamic-update-slice(f32[4,128,2,16,64]{1,0,4,3,2:T(4,128)} %get-tuple-element.1492, f32[1,128,2,16,64]{1,0,4,3,2:T(1,128)S(1)} %bitcast.617, s32[]{:T(128)} %get-tuple-element.1490, s32[]{:T(128)} %constant.207.clone.1..sunk.3, s32[]{:T(128)} %constant.207.clone.1..sunk.3, s32[]{:T(128)} %constant.207.clone.1..sunk.3, ...) | dynamic-update-slice | bytes 2097156 | tf_op jit(solution)/shard_map/jvp()/while/body/jit(dynamic_update_index_in_dim)/dynamic_update_slice | solution.py:102
  258.9 26.4 %dynamic_update_slice.79 = f32[4,128,2,16,64]{1,0,4,3,2:T(4,128)} dynamic-update-slice(f32[4,128,2,16,64]{1,0,4,3,2:T(4,128)} %get-tuple-element.1492, f32[1,128,2,16,64]{1,0,4,3,2:T(1,128)S(1)} %bitcast.617, s32[]{:T(128)} %get-tuple-element.1490, s32[]{:T(128)} %constant.207.clone.1..sunk.3, s32[]{:T(128)} %constant.207.clone.1..sunk.3, s32[]{:T(128)} %constant.207.clone.1..sunk.3, ...) | dynamic-update-slice | bytes 2097156 | tf_op jit(solution)/shard_map/jvp()/while/body/jit(dynamic_update_index_in_dim)/dynamic_update_slice | solution.py:102
  311.7 21.8 %all_gather.22 = f32[16,2,16]{2,1,0:T(2,128)S(1)} all-gather(f32[1,2,16]{2,1,0:T(2,128)S(1)} %fusion.149), channel_id=1, replica_groups=mesh['dp'=2,'ctx'=16,'head'=4] {'ctx'}, dimensions={0}, use_global_device_ids=true | all-gather | bytes 2176 | tf_op jit(solution)/shard_map/all_gather | solution.py:28
  342.3 6.6 reshape.478
  354.3 53.6 %all-gather.5.cloned.1.call-done = f32[32,16,128,64]{2,3,1,0:T(8,128)} async-done(((f32[2,16,128,64]{2,3,1,0:T(8,128)}), f32[32,16,128,64]{2,3,1,0:T(8,128)}) %all-gather.5.cloned.1.call-update) | async-done | bytes 16777232 | tf_op jit(solution)/shard_map/all_gather | solution.py:28
  421.8 7.4 copy.589
  435.0 8.6 fusion.108
  467.5 168.3 %all-gather.7.cloned.1.call-done = f32[32,16,128,64]{2,3,1,0:T(8,128)} async-done(((f32[2,16,128,64]{2,3,1,0:T(8,128)}), f32[32,16,128,64]{2,3,1,0:T(8,128)}) %all-gather.7.cloned.1.call-update) | async-done | bytes 16777232 | tf_op jit(solution)/shard_map/all_gather | solution.py:28
  637.4 76.6 %while.69 = (s32[]{:T(128)}, f32[2,16,128,64]{3,2,1,0:T(8,128)}, s32[]{:T(128)}, f32[16,2,16]{2,1,0:T(2,128)S(1)}, f32[16,2,16,128,64]{3,4,2,1,0:T(8,128)}, /*index=5*/s32[]{:T(128)}, s32[]{:T(128)}, s32[]{:T(128)}, s32[]{:T(128)}) while((s32[]{:T(128)}, f32[2,16,128,64]{3,2,1,0:T(8,128)}, s32[]{:T(128)}, f32[16,2,16]{2,1,0:T(2,128)S(1)}, ...), condition=%wide.region_10.11_spmd, body=%wide.region_9.10_spmd.sunk | while | flops 524294 | bytes 7340563 | solution.py:37
  720.6 9.9 reduce-window.16
  737.2 326.4 %while.70 = (s32[]{:T(128)}, f32[2,16,128,64]{2,3,1,0:T(8,128)S(1)}, f32[4,128,2,16,64]{1,0,4,3,2:T(4,128)}, f32[4,128,2,128]{1,0,3,2:T(4,128)}, f32[4,128,2,128...) while((s32[]{:T(128)}, ...), condition=%wide.region_21.22_spmd, body=%wide.region_11.21_spmd.sunk | while | flops 2103861760 | bytes 38124700 | solution.py:102
  788.5 26.4 %dynamic_update_slice.75 = f32[4,128,2,16,64]{1,0,4,3,2:T(4,128)} dynamic-update-slice(f32[4,128,2,16,64]{1,0,4,3,2:T(4,128)} %get-tuple-element.1588, f32[1,128,2,16,64]{1,0,4,3,2:T(1,128)S(1)} %bitcast.618, s32[]{:T(128)S(6)} %sub.275, s32[]{:T(128)} %constant.207.clone.1..sunk.2, s32[]{:T(128)} %constant.207.clone.1..sunk.2, s32[]{:T(128)} %constant.207.clone.1..sunk.2, s32[]{:T(128)} %constant.207.clone.1..sunk.2) | dynamic-update-slice | bytes 2097156 | tf_op jit(solution)/shard_map/transpose(jvp())/while/body/jit(dynamic_update_index_in_dim)/dynamic_update_slice | solution.py:102
  870.0 26.4 %dynamic_update_slice.75 = f32[4,128,2,16,64]{1,0,4,3,2:T(4,128)} dynamic-update-slice(f32[4,128,2,16,64]{1,0,4,3,2:T(4,128)} %get-tuple-element.1588, f32[1,128,2,16,64]{1,0,4,3,2:T(1,128)S(1)} %bitcast.618, s32[]{:T(128)S(6)} %sub.275, s32[]{:T(128)} %constant.207.clone.1..sunk.2, s32[]{:T(128)} %constant.207.clone.1..sunk.2, s32[]{:T(128)} %constant.207.clone.1..sunk.2, s32[]{:T(128)} %constant.207.clone.1..sunk.2) | dynamic-update-slice | bytes 2097156 | tf_op jit(solution)/shard_map/transpose(jvp())/while/body/jit(dynamic_update_index_in_dim)/dynamic_update_slice | solution.py:102
  951.5 26.4 %dynamic_update_slice.75 = f32[4,128,2,16,64]{1,0,4,3,2:T(4,128)} dynamic-update-slice(f32[4,128,2,16,64]{1,0,4,3,2:T(4,128)} %get-tuple-element.1588, f32[1,128,2,16,64]{1,0,4,3,2:T(1,128)S(1)} %bitcast.618, s32[]{:T(128)S(6)} %sub.275, s32[]{:T(128)} %constant.207.clone.1..sunk.2, s32[]{:T(128)} %constant.207.clone.1..sunk.2, s32[]{:T(128)} %constant.207.clone.1..sunk.2, s32[]{:T(128)} %constant.207.clone.1..sunk.2) | dynamic-update-slice | bytes 2097156 | tf_op jit(solution)/shard_map/transpose(jvp())/while/body/jit(dynamic_update_index_in_dim)/dynamic_update_slice | solution.py:102
  1033.0 26.4 %dynamic_update_slice.75 = f32[4,128,2,16,64]{1,0,4,3,2:T(4,128)} dynamic-update-slice(f32[4,128,2,16,64]{1,0,4,3,2:T(4,128)} %get-tuple-element.1588, f32[1,128,2,16,64]{1,0,4,3,2:T(1,128)S(1)} %bitcast.618, s32[]{:T(128)S(6)} %sub.275, s32[]{:T(128)} %constant.207.clone.1..sunk.2, s32[]{:T(128)} %constant.207.clone.1..sunk.2, s32[]{:T(128)} %constant.207.clone.1..sunk.2, s32[]{:T(128)} %constant.207.clone.1..sunk.2) | dynamic-update-slice | bytes 2097156 | tf_op jit(solution)/shard_map/transpose(jvp())/while/body/jit(dynamic_update_index_in_dim)/dynamic_update_slice | solution.py:102
  1075.9 6.2 multiply_add_fusion.1
  1087.1 8.8 multiply_reduce_fusion.7
  1109.8 9.7 pad_add_fusion
  1150.1 126.0 %all-reduce.18 = (bf16[5,2560]{1,0:T(8,128)(2,1)S(1)}, bf16[2048]{0:T(1024)(128)(2,1)S(1)}, bf16[3,32]{1,0:T(4,128)(2,1)S(1)}) all-reduce(bf16[5,2560]{1,0:T(8,128)(2,1)S(1)} %add_convert_fusion.1, bf16[2048]{0:T(1024)(128)(2,1)S(1)} %copy-done.59, ...), channel_id=1, replica_groups=mesh['dp'=2,'ctx'=16,'head'=4] {'dp','ctx'}, use_global_device_ids=true, to_apply=%region_31.32 | all-reduce | flops 14944 | bytes 59776 | tf_op jit(solution)/shard_map/psum | solution.py:226
  (697 shorter events, 591.8 us)
Async XLA Ops:
  7.2 47.0 %copy-start.69 = (f32[3,32]{1,0:T(4,128)S(1)}, f32[3,32]{1,0:T(4,128)}, u32[]{:S(2)}) copy-start(f32[3,32]{1,0:T(4,128)} %param.24) | copy-start | bytes 1156
  7.2 48.3 %copy-start.55 = (bf16[1,128,128]{2,1,0:T(8,128)(2,1)S(1)}, bf16[1,128,128]{2,1,0:T(8,128)(2,1)}, u32[]{:S(2)}) copy-start(bf16[1,128,128]{2,1,0:T(8,128)(2,1)} %param.20) | copy-start | bytes 98308
  7.2 49.0 %copy-start.57 = (f32[5,2560]{1,0:T(8,128)S(1)}, f32[5,2560]{1,0:T(8,128)}, u32[]{:S(2)}) copy-start(f32[5,2560]{1,0:T(8,128)} %param.22) | copy-start | bytes 153604
  11.6 50.0 %all-to-all-start.2 = ((bf16[128,4,2560]{0,2,1:T(8,128)(2,1)}), bf16[128,4,2560]{0,2,1:T(8,128)(2,1)}, u32[]{:S(2)}, u32[]{:S(2)}) async-start(bf16[128,4,2560]{0,2,1:T(8,128)(2,1)} %bitcast.54), calls=%async_computation.2 | async-start | bytes 5242880 | tf_op jit(solution)/shard_map/all_to_all | solution.py:182
  51.1 5.3 collective-permute-start
  61.7 10.5 all-to-all-start.1
  65.0 342.9 %all-gather.5.cloned.1.call-start = ((), (), s32[]{:S(2)}) async-start(), calls=%async_computation.7 | async-start | bytes 17825792 | tf_op jit(solution)/shard_map/all_gather | solution.py:28
  69.0 4.9 collective-permute-start.1
  295.9 37.5 %all-to-all-start = ((bf16[128,4,2048]{2,0,1:T(8,128)(2,1)}), bf16[128,4,2048]{2,0,1:T(8,128)(2,1)S(1)}, u32[]{:S(2)}, u32[]{:S(2)}) async-start(bf16[128,4,2048]{2,0,1:T(8,128)(2,1)} %copy.564), calls=%async_computation | async-start | bytes 4194304 | tf_op jit(solution)/shard_map/all_to_all | solution.py:185
  311.0 132.7 %copy-start.23 = (f32[512,2,16]{0,2,1:T(8,128)}, f32[512,2,16]{0,2,1:T(8,128)S(1)}, u32[]{:S(2)}) copy-start(f32[512,2,16]{0,2,1:T(8,128)S(1)} %copy.586) | copy-start | bytes 196612
  333.5 83.4 %all-to-all-start.3 = ((bf16[128,4,2048]{0,2,1:T(8,128)(2,1)}), bf16[128,4,2048]{0,2,1:T(8,128)(2,1)}, u32[]{:S(2)}, u32[]{:S(2)}) async-start(bf16[128,4,2048]{0,2,1:T(8,128)(2,1)} %bitcast.626), calls=%async_computation.3 | async-start | bytes 4194304 | tf_op jit(solution)/shard_map/all_to_all | solution.py:183
  337.9 297.9 %all-gather.7.cloned.1.call-start = ((), (), s32[]{:S(2)}) async-start(), calls=%async_computation.8 | async-start | bytes 17825792 | tf_op jit(solution)/shard_map/all_gather | solution.py:28
  463.1 668.6 %all-to-all-start.5 = ((bf16[4,128,2048]{1,2,0:T(8,128)(2,1)}), bf16[4,128,2048]{1,2,0:T(8,128)(2,1)}, u32[]{:S(2)}, u32[]{:S(2)}) async-start(bf16[4,128,2048]{1,2,0:T(8,128)(2,1)} %copy_bitcast_fusion.2), calls=%async_computation.5 | async-start | bytes 4194304 | tf_op jit(solution)/shard_map/all_to_all | solution.py:222
  780.6 34.3 %copy-start.25 = (f32[2,16]{1,0:T(2,128)S(1)}, f32[2,16]{1,0:T(2,128)}, u32[]{:S(2)}) copy-start(f32[2,16]{1,0:T(2,128)} %get-tuple-element.1450) | copy-start | bytes 388 | tf_op jit(solution)/shard_map/transpose(jvp())/while
  780.6 34.9 %copy-start.17 = (f32[128,2,16]{0,2,1:T(8,128)S(1)}, f32[128,2,16]{0,2,1:T(8,128)}, u32[]{:S(2)}) copy-start(f32[128,2,16]{0,2,1:T(8,128)} %copy-done.16) | copy-start | bytes 49156 | tf_op jit(solution)/shard_map/transpose(jvp())/while
  862.1 34.3 %copy-start.25 = (f32[2,16]{1,0:T(2,128)S(1)}, f32[2,16]{1,0:T(2,128)}, u32[]{:S(2)}) copy-start(f32[2,16]{1,0:T(2,128)} %get-tuple-element.1450) | copy-start | bytes 388 | tf_op jit(solution)/shard_map/transpose(jvp())/while
  862.1 34.9 %copy-start.17 = (f32[128,2,16]{0,2,1:T(8,128)S(1)}, f32[128,2,16]{0,2,1:T(8,128)}, u32[]{:S(2)}) copy-start(f32[128,2,16]{0,2,1:T(8,128)} %copy-done.16) | copy-start | bytes 49156 | tf_op jit(solution)/shard_map/transpose(jvp())/while
  943.6 34.3 %copy-start.25 = (f32[2,16]{1,0:T(2,128)S(1)}, f32[2,16]{1,0:T(2,128)}, u32[]{:S(2)}) copy-start(f32[2,16]{1,0:T(2,128)} %get-tuple-element.1450) | copy-start | bytes 388 | tf_op jit(solution)/shard_map/transpose(jvp())/while
  943.6 34.9 %copy-start.17 = (f32[128,2,16]{0,2,1:T(8,128)S(1)}, f32[128,2,16]{0,2,1:T(8,128)}, u32[]{:S(2)}) copy-start(f32[128,2,16]{0,2,1:T(8,128)} %copy-done.16) | copy-start | bytes 49156 | tf_op jit(solution)/shard_map/transpose(jvp())/while
  1025.1 34.3 %copy-start.25 = (f32[2,16]{1,0:T(2,128)S(1)}, f32[2,16]{1,0:T(2,128)}, u32[]{:S(2)}) copy-start(f32[2,16]{1,0:T(2,128)} %get-tuple-element.1450) | copy-start | bytes 388 | tf_op jit(solution)/shard_map/transpose(jvp())/while
  1025.1 34.9 %copy-start.17 = (f32[128,2,16]{0,2,1:T(8,128)S(1)}, f32[128,2,16]{0,2,1:T(8,128)}, u32[]{:S(2)}) copy-start(f32[128,2,16]{0,2,1:T(8,128)} %copy-done.16) | copy-start | bytes 49156 | tf_op jit(solution)/shard_map/transpose(jvp())/while
  1108.4 13.5 %collective-permute-start.2 = (f32[3,2560]{1,0:T(4,128)S(1)}, f32[3,2560]{1,0:T(4,128)S(1)}, u32[]{:S(2)}, u32[]{:S(2)}) collective-permute-start(f32[3,2560]{1,0:T(4,128)S(1)} %copy.604), channel_id=1, source_target_pairs={{4,0},{8,4},{12,8},{16,12},{20,16},{24,20},{28,24},{32,28},{36,32}... | collective-permute-start | bytes 92168 | tf_op jit(solution)/shard_map/ppermute | solution.py:21
  1131.7 8.5 all-to-all-start.6
  1140.1 138.5 %all-to-all-start.4 = ((bf16[4,128,2560]{1,2,0:T(8,128)(2,1)}), bf16[4,128,2560]{1,2,0:T(8,128)(2,1)S(1)}, u32[]{:S(2)}, u32[]{:S(2)}) async-start(bf16[4,128,2560]{1,2,0:T(8,128)(2,1)} %copy_bitcast_fusion.1), calls=%async_computation.4 | async-start | bytes 5242880 | tf_op jit(solution)/shard_map/all_to_all | solution.py:221
  (109 other events, 959.2 us)
Sparse Core Ops, SparseCore 0:
  290.2 117.6 all-gather.4
  449.9 185.9 all-gather.6
where the time goes:
time: 1310 us; the launch traced here: 1290 us
  local copies, waits for them, and re-layouts  481 us (37%)
  other arithmetic  228 us (17%)
  waiting for transfers between devices  224 us (17%)
  blocking collectives  181 us (14%)
  matrix products  119 us (9%)
  starting transfers between devices  38.1 us (3%)
  between operations  15.4 us (1%)
    dynamic_update_slice x28, local copies, waits for them, and re-layouts, scanned_spans(): lax.scan(jax.checkpoint(span_step), start_state, (split_up(x_part), split...  252 us
    all_gather x2, waiting for transfers between devices, prefix(): gathered = jax.tree.map(lambda a: lax.all_gather(a, axis), part)  222 us
    psum x1, blocking collectives, body(): lax.psum(grad_conv.astype(jnp.bfloat16), ('dp', 'ctx')).astype(jnp.float32)  126 us
    add x15, other arithmetic, compose(): decay_two[..., None, None] * state_one + state_two  47.7 us
    dot_general x12, matrix products, span_step(): y_part = jnp.einsum('gjts,sgjp->tgjp', weights, x_part, precision=triple)  46 us
    unnamed x132, local copies, waits for them, and re-layouts  35.4 us
    all_gather x1, blocking collectives, body(): seg_block = lax.all_gather(segment_ids, 'head', axis=1, tiled=True)[0]  32.9 us
    squeeze x24, local copies, waits for them, and re-layouts, scanned_spans(): lax.scan(jax.checkpoint(span_step), start_state, (split_up(x_part), split...  29.3 us
  transfers between devices with their start and end apart: 12, of which 3 were waited for; matrix products, arithmetic and copies ran while one was open for 44% of the time, Pallas kernels for 0%

commit v1 on v0

v1 whole, which is shorter than its diff:
```python
import jax
import jax.numpy as jnp
from jax import lax
from jax.experimental import pallas as pl
from jax.experimental.pallas import tpu as pltpu
from jax.sharding import PartitionSpec as P

HEADS = 128
GROUPS = 8
T = 128
GW = 1280
XW = 1024
CH = 10240
HP = 8192
LOG2E = 1.4426950408889634
EPS = 1e-05
NEG = -1e30

f32 = jnp.float32
bf16 = jnp.bfloat16
NN = ((1,), (0,))
NT = ((1,), (1,))
TN = ((0,), (0,))


def mm(a, b, dims=NN, precision=None):
    return lax.dot_general(a, b, (dims, ((), ())), preferred_element_type=f32, precision=precision)


def iota(shape, dim):
    return lax.broadcasted_iota(jnp.int32, shape, dim)


def sigmoid(v):
    return 0.5 * jnp.tanh(0.5 * v) + 0.5


def split(v):
    hi = v.astype(bf16)
    return hi, (v - hi.astype(f32)).astype(bf16)


def selector(g):
    return (iota((HEADS, XW), 0) == 16 * g + iota((HEADS, XW), 1) // 64).astype(f32).astype(bf16)


def twice(sel):
    return jnp.concatenate([sel, sel], axis=0)


def head_sums(v, sel):
    hi, lo = split(v)
    return mm(hi, sel, NT) + mm(lo, sel, NT)


def load_ext(ext, xbc_ref, halo_ref):
    ext[8:136, :] = xbc_ref[...].astype(f32)
    ext[5:8, :] = halo_ref[...].astype(f32)


def windows(ext, prep_ref, lanes):
    return [
        ext[5:133, lanes] * prep_ref[6],
        ext[6:134, lanes] * prep_ref[7],
        ext[7:135, lanes] * prep_ref[8],
        ext[8:136, lanes],
    ]


def conv(taps, wc_ref, lanes):
    pre = wc_ref[0, 4:5, lanes] + wc_ref[0, 3:4, lanes] * taps[3]
    for k in range(3):
        pre = pre + wc_ref[0, k : k + 1, lanes] * taps[k]
    return pre


def params(hp_ref, row):
    return jnp.concatenate([hp_ref[q, 5:6, 32 * row : 32 * row + 32] for q in range(4)], axis=1)


def make_prep(hseg_ref, hp_ref, dt_ref, seg_ref, prep_ref, pb_ref, segs):
    rate = jnp.exp(params(hp_ref, 0))
    dtb = dt_ref[...].astype(f32) + params(hp_ref, 1)
    step = jnp.maximum(dtb, 0.0) + jnp.log1p(jnp.exp(-jnp.abs(dtb)))
    decay = -step * rate
    rows, cols = iota((T, T), 0), iota((T, T), 1)
    low = (rows >= cols).astype(f32)
    run = mm(low, decay, NN, lax.Precision.HIGHEST) * LOG2E
    less = run - jnp.log(step) * LOG2E
    seg_row = jnp.broadcast_to(seg_ref[...].astype(f32) + 1.0, (T, T))
    seg_col = seg_row.T
    segs[8:136, :] = seg_col
    segs[5:8, :] = hseg_ref[...].astype(f32)
    prep_ref[0] = run
    prep_ref[1] = less
    prep_ref[2] = run.T
    prep_ref[3] = less.T
    same = seg_col == seg_row
    prep_ref[4] = jnp.where(same & (rows >= cols), 0.0, NEG)
    prep_ref[5] = jnp.where(same & (rows <= cols), 0.0, NEG)
    for k in range(3):
        prep_ref[6 + k] = (segs[5 + k : 133 + k, :] == seg_col).astype(f32)
    prep_ref[9] = step
    prep_ref[10] = decay
    linked = (seg_col == segs[7:8, :]).astype(f32)
    alpha = jnp.exp2(run) * linked
    omega = jnp.exp2(run[T - 1 :] - run) * (seg_col == seg_col[T - 1 :]).astype(f32) * step
    keep = alpha[T - 1 :]
    prep_ref[11] = sigmoid(dtb)
    for i, v in enumerate((alpha, omega)):
        hi, lo = split(v)
        pb_ref[i, :, :T] = hi
        pb_ref[i, :, T:] = lo
    both = jnp.where(rows == 0, params(hp_ref, 2), keep)
    hi, lo = split(both)
    pb_ref[2, :, :T] = hi
    pb_ref[2, :, T:] = lo


def k1(
    xbc_ref, halo_ref, hseg_ref, wc_ref, hp_ref, dt_ref, seg_ref,
    act_ref, pay_ref, prep_ref, pb_ref, ext, segs,
):
    g = pl.program_id(0)

    @pl.when(g == 0)
    def _():
        make_prep(hseg_ref, hp_ref, dt_ref, seg_ref, prep_ref, pb_ref, segs)

    load_ext(ext, xbc_ref, halo_ref)
    for c in range(GW // 128):
        lanes = slice(128 * c, 128 * c + 128)
        pre = conv(windows(ext, prep_ref, lanes), wc_ref, lanes)
        act_ref[:, lanes] = (pre * sigmoid(pre)).astype(bf16)
    sel = selector(g)
    omega = mm(pb_ref[1], twice(sel))
    weighted = (omega * act_ref[:, :XW].astype(f32)).astype(bf16)
    state = mm(act_ref[:, XW : XW + 128], weighted, TN).astype(bf16)
    khi = mm(pb_ref[2, :16, :T], sel)
    klo = mm(pb_ref[2, :16, T:], sel)
    tail = jnp.where(iota((16, XW), 0) == 0, khi[1:2], klo[1:2]).astype(bf16)
    for i in range(8):
        lanes = slice(128 * i, 128 * i + 128)
        pay_ref[i, :128, :] = state[:, lanes]
        pay_ref[i, 128:, :] = tail[:, lanes]


def parts_of(act_ref):
    return act_ref.at[:, :XW], act_ref.at[:, XW : XW + 128], act_ref.at[:, XW + 128 :]


def halves(v):
    left = iota(v.shape, 1) < 64
    zero = jnp.zeros_like(v)
    return jnp.concatenate([jnp.where(left, v, zero), jnp.where(left, zero, v)], axis=0)


def k2a(act_ref, prep_ref, y_ref):
    g = pl.program_id(0)
    x_ref, b_ref, c_ref = parts_of(act_ref)
    scores = mm(c_ref[...], b_ref[...], NT)
    run = pltpu.roll(prep_ref[0], (128 - 16 * g) % 128, 1)
    less = prep_ref[3, pl.ds(pl.multiple_of(16 * g, 16), 16), :]
    bias = prep_ref[4]
    for pair in range(8):
        mats = []
        for j in (2 * pair, 2 * pair + 1):
            el = jnp.exp2(run[:, j : j + 1] - less[j : j + 1, :] + bias)
            mats.append((el * scores).astype(bf16))
        lanes = slice(128 * pair, 128 * pair + 128)
        y_ref[:, lanes] = mm(jnp.concatenate(mats, axis=1), halves(x_ref[:, lanes]))


def scan_up(got_ref, start_ref):
    def one(j, state):
        start_ref[j] = state.astype(bf16)
        tail = got_ref[j, 128:, :].astype(f32)
        keep = tail[0:1] + tail[1:2]
        return keep * state + got_ref[j, :128, :].astype(f32)

    lax.fori_loop(0, 64, one, jnp.zeros((128, 128), f32))


def scan_down(tails_ref, got_ref, end_ref):
    def one(i, grad):
        j = 63 - i
        end_ref[j] = grad.astype(bf16)
        tail = tails_ref[j].astype(f32)
        keep = tail[0:1] + tail[1:2]
        return keep * grad + got_ref[j].astype(f32)

    lax.fori_loop(0, 64, one, jnp.zeros((128, 128), f32))


def wide(slots_ref):
    return jnp.concatenate([slots_ref[i] for i in range(8)], axis=1)


def k2b(
    act_ref, yi_ref, start_ref, gate_ref, cot_ref, gain_ref, pb_ref,
    dy_ref, dgate_ref, pay_ref, dcc_ref, rsum_ref, dgain_ref, dskip_ref,
    alpha_s, cs_s, ady_s, qhi_s, qlo_s,
):
    g = pl.program_id(0)
    x_ref, _, c_ref = parts_of(act_ref)

    @pl.when(g == 0)
    def _():
        rsum_ref[...] = jnp.zeros_like(rsum_ref)
        dskip_ref[...] = jnp.zeros_like(dskip_ref)

    sel = selector(g)
    both = twice(sel)
    start = wide(start_ref)
    cs_s[...] = mm(c_ref[...], start)
    alpha_s[...] = mm(pb_ref[0], both)
    skip = mm(pb_ref[2, :16, :], both)[0:1]
    gain = gain_ref[0, 5:6, :]
    dgain = jnp.zeros((16, XW), f32)
    dskip = jnp.zeros((16, XW), f32)
    for r in range(8):
        rows = slice(16 * r, 16 * r + 16)
        alpha = alpha_s[rows, :]
        yssm = yi_ref[rows, :] + alpha * cs_s[rows, :]
        x = x_ref[rows, :].astype(f32)
        ssm = (yssm + skip * x).astype(bf16).astype(f32)
        gate = gate_ref[rows, :].astype(f32)
        sg = sigmoid(gate)
        sl = gate * sg
        gated = ssm * sl
        rr = lax.rsqrt(jnp.sum(gated * gated, axis=1, keepdims=True) * (1.0 / XW) + EPS)
        norm = gated * rr
        cot = cot_ref[rows, :].astype(f32)
        dgain = dgain + cot * norm
        dn = cot * gain
        m2 = jnp.sum(dn * norm, axis=1, keepdims=True) * (1.0 / XW)
        dgated = rr * (dn - norm * m2)
        dy = (dgated * sl).astype(bf16)
        dy_ref[rows, :] = dy
        dgate_ref[rows, :] = (dgated * ssm * (sg + sl * (1.0 - sg))).astype(bf16)
        dyf = dy.astype(f32)
        ady_s[rows, :] = (alpha * dyf).astype(bf16)
        hi, lo = split(dyf * yssm)
        qhi_s[rows, :] = hi
        qlo_s[rows, :] = lo
        dskip = dskip + dyf * x
    ady = ady_s[...]
    dstart = mm(c_ref[...], ady, TN).astype(bf16)
    for i in range(8):
        pay_ref[i] = dstart[:, 128 * i : 128 * i + 128]
    dcc_ref[0] = mm(ady, start, NT)
    rsum_ref[...] += mm(qhi_s[...], sel, NT) + mm(qlo_s[...], sel, NT)
    dskip_ref[...] += head_sums(dskip, sel)
    dgain_ref[0] = jnp.sum(dgain, axis=0, keepdims=True)


def k3a(act_ref, dy_ref, prep_ref, dcc_ref, dx_ref, db_ref, dc_ref):
    g = pl.program_id(0)
    x_ref, b_ref, c_ref = parts_of(act_ref)
    scores = mm(b_ref[...], c_ref[...], NT)
    less = pltpu.roll(prep_ref[1], (128 - 16 * g) % 128, 1)
    run = prep_ref[2, pl.ds(pl.multiple_of(16 * g, 16), 16), :]
    bias = prep_ref[5]
    dscores = jnp.zeros((T, T), f32)
    for pair in range(8):
        lanes = slice(128 * pair, 128 * pair + 128)
        dy2 = halves(dy_ref[:, lanes])
        dmat = mm(x_ref[:, lanes], dy2, NT)
        mats = []
        for i in range(2):
            j = 2 * pair + i
            el = jnp.exp2(run[j : j + 1, :] - less[:, j : j + 1] + bias)
            mats.append((el * scores).astype(bf16))
            dscores = dscores + el * dmat[:, 128 * i : 128 * i + 128]
        dx_ref[:, lanes] = mm(jnp.concatenate(mats, axis=1), dy2)
    ds = dscores.astype(bf16)
    db_ref[0] = mm(ds, c_ref[...])
    dc_ref[0] = dcc_ref[0] + mm(ds, b_ref[...], TN)


def k3b(
    xbc_ref, halo_ref, wc_ref, hp_ref, act_ref, dy_ref, dxi_ref, dbi_ref, dci_ref,
    start_ref, pay_ref, end_ref, prep_ref, pb_ref, rsum_ref, dskip_ref,
    dxbc_ref, tail_ref, rim_ref, dconv_ref, ddt_ref, dhead_ref,
    ext, dact, csum, ksum,
):
    g = pl.program_id(0)

    @pl.when(g == 0)
    def _():
        csum[...] = jnp.zeros_like(csum)
        ksum[...] = jnp.zeros_like(ksum)

    sel = selector(g)
    both = twice(sel)
    b = act_ref[:, XW : XW + 128]
    end = wide(end_ref)
    rows16 = mm(pb_ref[2, :16, :], both)
    skip, keep = rows16[0:1], rows16[1:2]
    omega = mm(pb_ref[1], both)
    x = act_ref[:, :XW].astype(f32)
    dxs = dxi_ref[...] + omega * mm(b, end)
    csum[...] += head_sums(x * dxs, sel)
    dact[:, :XW] = (dxs + skip * dy_ref[...].astype(f32)).astype(bf16)
    dact[:, XW : XW + 128] = (dbi_ref[0] + mm((omega * x).astype(bf16), end, NT)).astype(bf16)
    dact[:, XW + 128 :] = dci_ref[0].astype(bf16)
    final = keep * wide(start_ref).astype(f32) + wide(pay_ref).astype(f32)
    part = jnp.sum((final * end.astype(f32)).reshape(16, 8, XW), axis=0)
    ksum[...] += head_sums(part, sel)

    load_ext(ext, xbc_ref, halo_ref)
    rows = iota((T, 128), 0)
    for c in range(GW // 128):
        lanes = slice(128 * c, 128 * c + 128)
        taps = windows(ext, prep_ref, lanes)
        pre = conv(taps, wc_ref, lanes)
        sg = sigmoid(pre)
        dpre = dact[:, lanes].astype(f32) * (sg + pre * sg * (1.0 - sg))
        for k in range(4):
            dconv_ref[0, k : k + 1, lanes] = jnp.sum(dpre * taps[k], axis=0, keepdims=True)
        dconv_ref[0, 4:5, lanes] = jnp.sum(dpre, axis=0, keepdims=True)
        total = wc_ref[0, 3:4, lanes] * dpre
        rim = jnp.zeros((8, 128), f32)
        for k in range(3):
            far = 3 - k
            moved = pltpu.roll(wc_ref[0, k : k + 1, lanes] * dpre * prep_ref[6 + k], T - far, 0)
            inside = rows < T - far
            total = total + jnp.where(inside, moved, 0.0)
            rim = rim + jnp.where(inside, 0.0, moved)[T - 8 :]
        dxbc_ref[:, lanes] = total.astype(bf16)
        tail_ref[:, lanes] = total[T - 8 :]
        rim_ref[:, lanes] = rim

    @pl.when(g == GROUPS - 1)
    def _():
        high = (iota((T, T), 0) <= iota((T, T), 1)).astype(f32)
        step, decay = prep_ref[9], prep_ref[10]
        col = csum[...]
        dlog = mm(high, rsum_ref[...] - col, NN, lax.Precision.HIGHEST)
        dlog = dlog + jnp.sum(ksum[...], axis=0, keepdims=True)
        dstep = col / step - dlog * jnp.exp(params(hp_ref, 0))
        ddt = dstep * prep_ref[11]
        ddt_ref[...] = ddt.astype(bf16)
        dhead_ref[0:1, :] = jnp.sum(dlog * decay, axis=0, keepdims=True)
        dhead_ref[1:2, :] = jnp.sum(ddt, axis=0, keepdims=True)
        dhead_ref[2:3, :] = jnp.sum(dskip_ref[...], axis=0, keepdims=True)
        dhead_ref[3:8, :] = jnp.zeros((5, HEADS), f32)


def S(shape, dtype):
    return jax.ShapeDtypeStruct(shape, dtype)


def fixed(shape):
    return pl.BlockSpec(shape, lambda g: (0,) * len(shape))


def lane_block(rows, width):
    return pl.BlockSpec((rows, width), lambda g: (0, g))


def slot_block(*shape):
    return pl.BlockSpec(shape, lambda g: (g,) + (0,) * (len(shape) - 1))


WC_SPEC = pl.BlockSpec((1, 6, GW), lambda g: (g // 2, 0, g % 2))
GAIN_SPEC = pl.BlockSpec((1, 6, XW), lambda g: (g // 2, 0, g % 2))
HP_SPEC = pl.BlockSpec((4, 6, 128), lambda g: (0, 0, 16))


def call(kernel, name, ins, in_specs, outs, out_specs, scratch=(), cost=0, grid=(GROUPS,)):
    return pl.pallas_call(
        kernel,
        grid=grid,
        in_specs=in_specs,
        out_specs=out_specs,
        out_shape=outs,
        scratch_shapes=scratch,
        compiler_params=pltpu.CompilerParams(vmem_limit_bytes=48 << 20),
        cost_estimate=pl.CostEstimate(flops=cost, bytes_accessed=8 << 20, transcendentals=0),
        name=name,
    )(*ins)


def body(
    xbc_raw, gate_raw, dt_raw, segment_ids, conv_weight, norm_gain, head_params, out_cotangent
):
    xbc, gate, dt, cot = xbc_raw[0], gate_raw[0], dt_raw[0], out_cotangent[0]
    along = ("ctx", "head")
    count = lax.axis_size("ctx") * lax.axis_size("head")
    up = [(i, i + 1) for i in range(count - 1)]
    down = [(i + 1, i) for i in range(count - 1)]

    own_w = jnp.concatenate(
        [
            conv_weight,
            jnp.concatenate(
                [norm_gain[None], head_params.reshape(1, 96), jnp.zeros((1, 416), f32)], axis=1
            ),
        ],
        axis=0,
    )
    w_all = lax.all_to_all(
        jnp.broadcast_to(own_w[None], (4, 6, 2560)), "head", split_axis=0, concat_axis=0, tiled=True
    )
    last_ids = jnp.broadcast_to((segment_ids[0, T - 3 :] + 1).astype(bf16)[:, None], (3, 128))
    halo = lax.ppermute(jnp.concatenate([xbc[T - 3 :], last_ids], axis=1), along, up)

    act, pay, prep, pb = call(
        k1,
        "conv_states",
        (xbc, halo, halo, w_all, w_all, dt, segment_ids),
        [
            lane_block(T, GW),
            lane_block(3, GW),
            pl.BlockSpec((3, 128), lambda g: (0, CH // 128)),
            WC_SPEC,
            HP_SPEC,
            fixed((T, HEADS)),
            fixed((1, T)),
        ],
        (S((T, CH), bf16), S((64, 144, 128), bf16), S((12, T, T), f32), S((3, T, 2 * T), bf16)),
        (lane_block(T, GW), slot_block(8, 144, 128), fixed((12, T, T)), fixed((3, T, 2 * T))),
        (pltpu.VMEM((136, GW), f32), pltpu.VMEM((136, 128), f32)),
    )
    got = lax.all_to_all(pay, along, split_axis=0, concat_axis=0, tiled=True)

    yi = call(
        k2a,
        "inner_forward",
        (act, prep),
        [lane_block(T, GW), fixed((12, T, T))],
        S((T, HP), f32),
        lane_block(T, XW),
        cost=4 << 30,
    )
    starts = call(
        scan_up,
        "scan_up",
        (got,),
        [fixed((64, 144, 128))],
        S((64, 128, 128), bf16),
        fixed((64, 128, 128)),
        grid=(1,),
    )
    start = lax.all_to_all(starts, along, split_axis=0, concat_axis=0, tiled=True)

    dy, dgate, pay2, dcc, rsum, dgain, dskip = call(
        k2b,
        "gate_norm",
        (act, yi, start, gate, cot, w_all, pb),
        [
            lane_block(T, GW),
            lane_block(T, XW),
            slot_block(8, 128, 128),
            lane_block(T, XW),
            lane_block(T, XW),
            GAIN_SPEC,
            fixed((3, T, 2 * T)),
        ],
        (
            S((T, HP), bf16),
            S((T, HP), bf16),
            S((64, 128, 128), bf16),
            S((8, T, 128), f32),
            S((T, HEADS), f32),
            S((8, 1, XW), f32),
            S((16, HEADS), f32),
        ),
        (
            lane_block(T, XW),
            lane_block(T, XW),
            slot_block(8, 128, 128),
            slot_block(1, T, 128),
            fixed((T, HEADS)),
            slot_block(1, 1, XW),
            fixed((16, HEADS)),
        ),
        (
            pltpu.VMEM((T, XW), f32),
            pltpu.VMEM((T, XW), f32),
            pltpu.VMEM((T, XW), bf16),
            pltpu.VMEM((T, XW), bf16),
            pltpu.VMEM((T, XW), bf16),
        ),
    )
    got2 = lax.all_to_all(pay2, along, split_axis=0, concat_axis=0, tiled=True)
    dxi, dbi, dci = call(
        k3a,
        "inner_backward",
        (act, dy, prep, dcc),
        [lane_block(T, GW), lane_block(T, XW), fixed((12, T, T)), slot_block(1, T, 128)],
        (S((T, HP), f32), S((8, T, 128), f32), S((8, T, 128), f32)),
        (lane_block(T, XW), slot_block(1, T, 128), slot_block(1, T, 128)),
        cost=4 << 30,
    )
    ends = call(
        scan_down,
        "scan_down",
        (got, got2),
        [pl.BlockSpec((64, 16, 128), lambda g: (0, 8, 0)), fixed((64, 128, 128))],
        S((64, 128, 128), bf16),
        fixed((64, 128, 128)),
        grid=(1,),
    )
    end = lax.all_to_all(ends, along, split_axis=0, concat_axis=0, tiled=True)

    dxbc, tail, rim, dconv, ddt, dhead = call(
        k3b,
        "conv_backward",
        (xbc, halo, w_all, w_all, act, dy, dxi, dbi, dci, start, pay, end, prep, pb, rsum, dskip),
        [
            lane_block(T, GW),
            lane_block(3, GW),
            WC_SPEC,
            HP_SPEC,
            lane_block(T, GW),
            lane_block(T, XW),
            lane_block(T, XW),
            slot_block(1, T, 128),
            slot_block(1, T, 128),
            slot_block(8, 128, 128),
            pl.BlockSpec((8, 128, 128), lambda g: (g, 0, 0)),
            slot_block(8, 128, 128),
            fixed((12, T, T)),
            fixed((3, T, 2 * T)),
            fixed((T, HEADS)),
            fixed((16, HEADS)),
        ],
        (
            S((T, CH), bf16),
            S((8, CH), f32),
            S((8, CH), f32),
            S((4, 5, 2560), f32),
            S((T, HEADS), bf16),
            S((8, HEADS), f32),
        ),
        (
            lane_block(T, GW),
            lane_block(8, GW),
            lane_block(8, GW),
            pl.BlockSpec((1, 5, GW), lambda g: (g // 2, 0, g % 2)),
            fixed((T, HEADS)),
            fixed((8, HEADS)),
        ),
        (
            pltpu.VMEM((136, GW), f32),
            pltpu.VMEM((T, GW), bf16),
            pltpu.VMEM((T, HEADS), f32),
            pltpu.VMEM((8, HEADS), f32),
        ),
    )
    rim_in = lax.ppermute(rim[5:].astype(bf16), along, down)
    last_rows = (tail[5:] + rim_in.astype(f32)).astype(bf16)
    grad_xbc = lax.dynamic_update_slice(dxbc, last_rows, (T - 3, 0))

    heads4 = dhead[:3].reshape(3, 4, 32).transpose(1, 0, 2).reshape(4, 96)
    parts = jnp.concatenate(
        [
            dconv.reshape(4, 5 * 2560),
            dgain.reshape(4, 2048),
            heads4,
            jnp.zeros((4, 16384 - 5 * 2560 - 2048 - 96), f32),
        ],
        axis=1,
    )
    pieces = parts.reshape(4, 2, 16, 512).transpose(1, 2, 0, 3).reshape(128, 4, 128)
    everyone = ("dp", "ctx", "head")
    mine = jnp.sum(
        lax.all_to_all(pieces, everyone, split_axis=0, concat_axis=0, tiled=True), axis=0
    )
    whole = lax.all_to_all(
        jnp.broadcast_to(mine[None], (32, 4, 128)),
        ("dp", "ctx"),
        split_axis=0,
        concat_axis=0,
        tiled=True,
    ).reshape(-1)
    return (
        grad_xbc[None],
        dgate[None],
        ddt[None],
        whole[: 5 * 2560].reshape(5, 2560),
        whole[5 * 2560 : 5 * 2560 + 2048],
        whole[5 * 2560 + 2048 : 5 * 2560 + 2144].reshape(3, 32),
    )


def solution(mesh):
    token = P("dp", ("ctx", "head"), None)
    return jax.shard_map(
        body,
        mesh=mesh,
        in_specs=(
            token, token, token, P("dp", ("ctx", "head")),
            P(None, "head"), P("head"), P(None, "head"), token,
        ),
        out_specs=(token, token, token, P(None, "head"), P("head"), P(None, "head")),
        check_vma=False,
    )
```

time: 1310 us -> 256 us (0.20); the launches traced: 1290 us -> 254 us
  local copies, waits for them, and re-layouts: 481 us -> 28 us
  other arithmetic: 228 us -> 1.96 us
  waiting for transfers between devices: 224 us -> 46.7 us
  matrix products: 119 us -> 0 us
  blocking collectives: 181 us -> 73.1 us
  Pallas kernels: 0 us -> 68.2 us
  between operations: 15.4 us -> 0.82 us
    dynamic_update_slice x28 -> x1, local copies, waits for them, and re-layouts: 252 us -> 2.1 us  [body(): grad_xbc = lax.dynamic_update_slice(dxbc, last_rows, (T - 3, 0))]
    all_gather x2 -> x0, waiting for transfers between devices: 222 us -> none  [prefix(): gathered = jax.tree.map(lambda a: lax.all_gather(a, axis), part)]
    psum x1 -> x0, blocking collectives: 126 us -> none  [body(): lax.psum(grad_conv.astype(jnp.bfloat16), ('dp', 'ctx')).astype(jnp.float32)]
    dot_general x55 -> x0, matrix products: 111 us -> none  [the longest x12 46 us: span_step(): y_part = jnp.einsum('gjts,sgjp->tgjp', weights, x_part, precision=triple)]
    all_to_all x0 -> x2, blocking collectives: none -> 73.1 us  [the longest x1 40.8 us: body(): got = lax.all_to_all(pay, along, split_axis=0, concat_axis=0, tiled=True)]
    pallas_call x0 -> x7, Pallas kernels: none -> 68.2 us  [call(): pl.pallas_call(kernel, grid=grid, in_specs=in_specs, out_specs=out_specs,...]
    dynamic_slice x50 -> x0, local copies, waits for them, and re-layouts: 54.7 us -> none  [the longest x30 28.5 us: one(): lax.dynamic_index_in_dim(a, source, 0, False)]
    all_gather x2 -> x0, blocking collectives: 54.7 us -> none  [the longest x1 32.9 us: body(): seg_block = lax.all_gather(segment_ids, 'head', axis=1, tiled=True)[0]]
  transfers between devices with their start and end apart: 12 -> 7, of which waited for: 3 -> 5; matrix products, arithmetic and copies ran while one was open for 44% -> 2% of each run, Pallas kernels for 0% -> 6%
where the time goes in v1:
time: 256 us; the launch traced here: 254 us
  blocking collectives  73.1 us (29%)
  Pallas kernels  68.2 us (27%)
  waiting for transfers between devices  46.7 us (18%)
  starting transfers between devices  35.7 us (14%)
  local copies, waits for them, and re-layouts  28 us (11%)
    pallas_call x7, Pallas kernels, call(): pl.pallas_call(kernel, grid=grid, in_specs=in_specs, out_specs=out_specs,...  68.2 us
    all_to_all x1, blocking collectives, body(): got = lax.all_to_all(pay, along, split_axis=0, concat_axis=0, tiled=True)  40.8 us
    all_to_all x1, blocking collectives, body(): got2 = lax.all_to_all(pay2, along, split_axis=0, concat_axis=0, tiled=True)  32.3 us
    all_to_all x1, waiting for transfers between devices, body(): lax.all_to_all(starts, along, split_axis=0, concat_axis=0, tiled=True)  17.8 us
    unnamed x43, local copies, waits for them, and re-layouts  17.7 us
    all_to_all x1, waiting for transfers between devices, body(): end = lax.all_to_all(ends, along, split_axis=0, concat_axis=0, tiled=True)  14.2 us
    all_to_all x1, starting transfers between devices, body(): lax.all_to_all(pieces, everyone, split_axis=0, concat_axis=0, tiled=True)  8.36 us
    all_to_all x1, waiting for transfers between devices, body(): lax.all_to_all(pieces, everyone, split_axis=0, concat_axis=0, tiled=True)  8.31 us
  transfers between devices with their start and end apart: 7, of which 5 were waited for; matrix products, arithmetic and copies ran while one was open for 2% of the time, Pallas kernels for 6%

profile of v1, /device:TPU:1, one launch (start us, length us, event | category | flops | bytes accessed | tf_op | source)
XLA Modules:
  0.0 254.5 jit_solution(10847073811810789701)
XLA Ops:
  3.8 5.9 %all-to-all-start = ((f32[4,6,2560]{2,1,0:T(8,128)}), f32[4,6,2560]{2,1,0:T(8,128)S(1)}, u32[]{:S(2)}, u32[]{:S(2)}) async-start(f32[4,6,2560]{2,1,0:T(8,128)} %broadcast_in_dim.41), calls=%async_computation | async-start | bytes 655360 | tf_op jit(solution)/shard_map/all_to_all | solution.py:403
  11.5 3.4 %collective-permute-start = (bf16[3,10368]{1,0:T(4,128)(2,1)S(1)}, bf16[3,10368]{1,0:T(4,128)(2,1)S(1)}, u32[]{:S(2)}, u32[]{:S(2)}) collective-permute-start(bf16[3,10368]{1,0:T(4,128)(2,1)S(1)} %pad_maximum_fusion), channel_id=1, source_target_pairs={{0,1},{1,2},{2,3},{3,4},{4,5},{5,6},{6,7},{7,8},{8,9},{9,10},{10,1... | collective-permute-start | bytes 186632 | tf_op jit(solution)/shard_map/ppermute | solution.py:407
  14.9 1.5 collective-permute-done.halo_ref.hseg_ref
  17.8 11.4 %conv_states.1 = (bf16[128,10240]{1,0:T(8,128)(2,1)}, bf16[64,144,128]{2,1,0:T(8,128)(2,1)S(1)}, f32[12,128,128]{2,1,0:T(8,128)S(1)}, bf16[3,128,256]{2,1,0:T(8,128)(2,1)S(1)}) custom-call(bf16[128,10240]{1,0:T(8,128)(2,1)} %bitcast.25, bf16[3,10368]{1,0:T(4,128)(2,1)S(1)} %collective-permute-done.halo_ref.hseg_ref, ...), custom_call_target="tpu_custom_call" | custom-call | bytes 8388608 | tf_op jit(solution)/shard_map/conv_states/pallas_call | solution.py:372
  29.2 1.5 copy-done.2
  30.7 40.8 %all_to_all.35.got_ref.tails_ref = bf16[64,144,128]{2,1,0:T(8,128)(2,1)S(1)} all-to-all(bf16[64,144,128]{2,1,0:T(8,128)(2,1)S(1)} %get-tuple-element.28.pay_ref), channel_id=1, replica_groups=mesh['dp'=2,'ctx'=16,'head'=4] {'ctx','head'}, dimensions={0} | all-to-all | bytes 4718592 | tf_op jit(solution)/shard_map/all_to_all | solution.py:426
  72.9 1.3 copy-done.3
  74.2 5.3 %all-to-all-start.2 = ((bf16[64,128,128]{2,1,0:T(8,128)(2,1)}), bf16[64,128,128]{2,1,0:T(8,128)(2,1)S(1)}, u32[]{:S(2)}, u32[]{:S(2)}) async-start(bf16[64,128,128]{2,1,0:T(8,128)(2,1)} %copy-done.3), calls=%async_computation.2 | async-start | bytes 4194304 | tf_op jit(solution)/shard_map/all_to_all | solution.py:446
  79.5 1.7 copy-done.1
  81.2 6.5 %inner_forward.1.yi_ref = f32[128,8192]{1,0:T(8,128)} custom-call(bf16[128,10240]{1,0:T(8,128)(2,1)S(1)} %copy-done.1, f32[12,128,128]{2,1,0:T(8,128)S(1)} %get-tuple-element.27.prep_ref), custom_call_target="tpu_custom_call" | custom-call | flops 4294967296 | bytes 8388608 | tf_op jit(solution)/shard_map/inner_forward/pallas_call | solution.py:372
  87.7 17.8 %all-to-all-done.2.start_ref = bf16[64,128,128]{2,1,0:T(8,128)(2,1)S(1)} async-done(((bf16[64,128,128]{2,1,0:T(8,128)(2,1)}), bf16[64,128,128]{2,1,0:T(8,128)(2,1)S(1)}, u32[]{:S(2)}, u32[]{:S(2)}) %all-to-all-start.2) | async-done | bytes 2097184 | tf_op jit(solution)/shard_map/all_to_all | solution.py:446
  105.5 1.3 copy-done.20
  106.8 14.6 %gate_norm.1 = (bf16[128,8192]{1,0:T(8,128)(2,1)S(1)}, bf16[128,8192]{1,0:T(8,128)(2,1)}, bf16[64,128,128]{2,1,0:T(8,128)(2,1)S(1)}, f32[8,128,128]{2,1,0:T(8,12...) custom-call(bf16[128,10240]{1,0:T(8,128)(2,1)} %get-tuple-element.26.act_ref, ...), custom_call_target="tpu_custom_call" | custom-call | bytes 8388608 | tf_op jit(solution)/shard_map/gate_norm/pallas_call | solution.py:372
  122.2 32.3 %all_to_all.36.got_ref = bf16[64,128,128]{2,1,0:T(8,128)(2,1)S(1)} all-to-all(bf16[64,128,128]{2,1,0:T(8,128)(2,1)S(1)} %get-tuple-element.35), channel_id=1, replica_groups=mesh['dp'=2,'ctx'=16,'head'=4] {'ctx','head'}, dimensions={0} | all-to-all | bytes 4194304 | tf_op jit(solution)/shard_map/all_to_all | solution.py:487
  154.5 2.9 %scan_down.1 = bf16[64,128,128]{2,1,0:T(8,128)(2,1)} custom-call(bf16[64,144,128]{2,1,0:T(8,128)(2,1)} %copy-done, bf16[64,128,128]{2,1,0:T(8,128)(2,1)S(1)} %all_to_all.36.got_ref), custom_call_target="tpu_custom_call" | custom-call | bytes 8388608 | tf_op jit(solution)/shard_map/scan_down/pallas_call | solution.py:372
  157.4 6.9 %all-to-all-start.4 = ((bf16[64,128,128]{2,1,0:T(8,128)(2,1)}), bf16[64,128,128]{2,1,0:T(8,128)(2,1)}, u32[]{:S(2)}, u32[]{:S(2)}) async-start(bf16[64,128,128]{2,1,0:T(8,128)(2,1)} %scan_down.1), calls=%async_computation.4 | async-start | bytes 4194304 | tf_op jit(solution)/shard_map/all_to_all | solution.py:506
  165.5 8.7 %inner_backward.1 = (f32[128,8192]{1,0:T(8,128)}, f32[8,128,128]{2,1,0:T(8,128)S(1)}, f32[8,128,128]{2,1,0:T(8,128)S(1)}) custom-call(bf16[128,10240]{1,0:T(8,128)(2,1)} %get-tuple-element.26.act_ref, bf16[128,8192]{1,0:T(8,128)(2,1)S(1)} %get-tuple-element.30.dy_ref, f32[12,128,128]{2,1,0:T(8,128)S(1)} %get-tuple-element.27.prep_ref, ...), custom_call_target="tpu_custom_call" | custom-call | flops 4294967296 | bytes 8388608 | tf_op jit(solution)/shard_map/inner_backward/pallas_call | solution.py:372
  175.8 14.2 %all-to-all-done.4.end_ref = bf16[64,128,128]{2,1,0:T(8,128)(2,1)} async-done(((bf16[64,128,128]{2,1,0:T(8,128)(2,1)}), bf16[64,128,128]{2,1,0:T(8,128)(2,1)}, u32[]{:S(2)}, u32[]{:S(2)}) %all-to-all-start.4) | async-done | bytes 2097184 | tf_op jit(solution)/shard_map/all_to_all | solution.py:506
  193.1 23.4 %conv_backward.1 = (bf16[128,10240]{1,0:T(8,128)(2,1)}, f32[8,10240]{1,0:T(8,128)S(1)}, f32[8,10240]{1,0:T(8,128)S(1)}, f32[4,5,2560]{2,1,0:T(8,128)S(1)}, bf16[...) custom-call(bf16[128,10240]{1,0:T(8,128)(2,1)} %bitcast.26, bf16[3,10368]{1,0:T(4,128)(2,1)S(1)} %copy-done.7, ...), custom_call_target="tpu_custom_call" | custom-call | bytes 8388608 | tf_op jit(solution)/shard_map/conv_backward/pallas_call | solution.py:372
  221.0 8.4 %all-to-all-start.5 = ((f32[128,4,128]{2,1,0:T(4,128)}), f32[128,4,128]{2,1,0:T(4,128)S(1)}, u32[]{:S(2)}, u32[]{:S(2)}) async-start(f32[128,4,128]{2,1,0:T(4,128)} %reshape.63), calls=%async_computation.5 | async-start | bytes 524288 | tf_op jit(solution)/shard_map/all_to_all | solution.py:570
  231.7 8.3 %all-to-all-done.5 = f32[128,4,128]{2,1,0:T(4,128)S(1)} async-done(((f32[128,4,128]{2,1,0:T(4,128)}), f32[128,4,128]{2,1,0:T(4,128)S(1)}, u32[]{:S(2)}, u32[]{:S(2)}) %all-to-all-start.5) | async-done | bytes 262176 | tf_op jit(solution)/shard_map/all_to_all | solution.py:570
  240.8 4.7 %all-to-all-start.6 = ((f32[32,4,128]{2,1,0:T(4,128)}), f32[32,4,128]{2,1,0:T(4,128)S(1)}, u32[]{:S(2)}, u32[]{:S(2)}) async-start(f32[32,4,128]{2,1,0:T(4,128)} %broadcast_in_dim.47), calls=%async_computation.6 | async-start | bytes 131072 | tf_op jit(solution)/shard_map/all_to_all | solution.py:572
  245.5 2.1 dynamic_update_slice.4
  247.6 4.9 %all-to-all-done.6 = f32[32,4,128]{2,1,0:T(4,128)S(1)} async-done(((f32[32,4,128]{2,1,0:T(4,128)}), f32[32,4,128]{2,1,0:T(4,128)S(1)}, u32[]{:S(2)}, u32[]{:S(2)}) %all-to-all-start.6) | async-done | bytes 65568 | tf_op jit(solution)/shard_map/all_to_all | solution.py:572
  (70 shorter events, 24.0 us)
Async XLA Ops:
  3.8 12.5 %all-to-all-start = ((f32[4,6,2560]{2,1,0:T(8,128)}), f32[4,6,2560]{2,1,0:T(8,128)S(1)}, u32[]{:S(2)}, u32[]{:S(2)}) async-start(f32[4,6,2560]{2,1,0:T(8,128)} %broadcast_in_dim.41), calls=%async_computation | async-start | bytes 655360 | tf_op jit(solution)/shard_map/all_to_all | solution.py:403
  11.5 4.9 %collective-permute-start = (bf16[3,10368]{1,0:T(4,128)(2,1)S(1)}, bf16[3,10368]{1,0:T(4,128)(2,1)S(1)}, u32[]{:S(2)}, u32[]{:S(2)}) collective-permute-start(bf16[3,10368]{1,0:T(4,128)(2,1)S(1)} %pad_maximum_fusion), channel_id=1, source_target_pairs={{0,1},{1,2},{2,3},{3,4},{4,5},{5,6},{6,7},{7,8},{8,9},{9,10},{10,1... | collective-permute-start | bytes 186632 | tf_op jit(solution)/shard_map/ppermute | solution.py:407
  16.4 12.8 %copy-start.6 = (bf16[3,10368]{1,0:T(4,128)(2,1)}, bf16[3,10368]{1,0:T(4,128)(2,1)S(1)}, u32[]{:S(2)}) copy-start(bf16[3,10368]{1,0:T(4,128)(2,1)S(1)} %collective-permute-done.halo_ref.hseg_ref) | copy-start | bytes 186628
  16.4 0.8 copy-start.15
  29.2 1.5 copy-start.2
  29.2 42.3 %copy-start.4 = (bf16[3,128,256]{2,1,0:T(8,128)(2,1)}, bf16[3,128,256]{2,1,0:T(8,128)(2,1)S(1)}, u32[]{:S(2)}) copy-start(bf16[3,128,256]{2,1,0:T(8,128)(2,1)S(1)} %get-tuple-element.29.pb_ref) | copy-start | bytes 589828
  71.5 1.4 copy-start
  72.9 1.3 copy-start.3
  74.2 31.3 %all-to-all-start.2 = ((bf16[64,128,128]{2,1,0:T(8,128)(2,1)}), bf16[64,128,128]{2,1,0:T(8,128)(2,1)S(1)}, u32[]{:S(2)}, u32[]{:S(2)}) async-start(bf16[64,128,128]{2,1,0:T(8,128)(2,1)} %copy-done.3), calls=%async_computation.2 | async-start | bytes 4194304 | tf_op jit(solution)/shard_map/all_to_all | solution.py:446
  79.5 1.7 copy-start.1
  81.2 25.6 %copy-start.5 = (bf16[3,128,256]{2,1,0:T(8,128)(2,1)S(1)}, bf16[3,128,256]{2,1,0:T(8,128)(2,1)}, u32[]{:S(2)}) copy-start(bf16[3,128,256]{2,1,0:T(8,128)(2,1)} %copy-done.4) | copy-start | bytes 589828
  105.5 1.3 copy-start.20
  121.4 0.8 copy-start.18
  157.4 32.7 %all-to-all-start.4 = ((bf16[64,128,128]{2,1,0:T(8,128)(2,1)}), bf16[64,128,128]{2,1,0:T(8,128)(2,1)}, u32[]{:S(2)}, u32[]{:S(2)}) async-start(bf16[64,128,128]{2,1,0:T(8,128)(2,1)} %scan_down.1), calls=%async_computation.4 | async-start | bytes 4194304 | tf_op jit(solution)/shard_map/all_to_all | solution.py:506
  164.4 1.0 copy-start.19
  174.2 0.8 copy-start.8
  175.0 0.8 copy-start.10
  190.1 0.9 copy-start.7
  191.0 1.0 copy-start.9
  192.0 1.0 copy-start.11
  218.6 26.8 %copy-start.14 = (f32[8,10240]{1,0:T(8,128)S(1)}, f32[8,10240]{1,0:T(8,128)}, u32[]{:S(2)}) copy-start(f32[8,10240]{1,0:T(8,128)} %copy-done.13) | copy-start | bytes 983044
  221.0 19.0 %all-to-all-start.5 = ((f32[128,4,128]{2,1,0:T(4,128)}), f32[128,4,128]{2,1,0:T(4,128)S(1)}, u32[]{:S(2)}, u32[]{:S(2)}) async-start(f32[128,4,128]{2,1,0:T(4,128)} %reshape.63), calls=%async_computation.5 | async-start | bytes 524288 | tf_op jit(solution)/shard_map/all_to_all | solution.py:570
  230.4 15.1 %collective-permute-start.1 = (bf16[3,10240]{1,0:T(4,128)(2,1)S(1)}, bf16[3,10240]{1,0:T(4,128)(2,1)S(1)}, u32[]{:S(2)}, u32[]{:S(2)}) collective-permute-start(bf16[3,10240]{1,0:T(4,128)(2,1)S(1)} %slice.56), channel_id=1, source_target_pairs={{1,0},{2,1},{3,2},{4,3},{5,4},{6,5},{7,6},{8,7},{9,8},{10,9},{11,1... | collective-permute-start | bytes 184328 | tf_op jit(solution)/shard_map/ppermute | solution.py:553
  240.8 11.8 %all-to-all-start.6 = ((f32[32,4,128]{2,1,0:T(4,128)}), f32[32,4,128]{2,1,0:T(4,128)S(1)}, u32[]{:S(2)}, u32[]{:S(2)}) async-start(f32[32,4,128]{2,1,0:T(4,128)} %broadcast_in_dim.47), calls=%async_computation.6 | async-start | bytes 131072 | tf_op jit(solution)/shard_map/all_to_all | solution.py:572
  (4 other events, 2.8 us)

commit v2 on v1

v2 whole, which is shorter than its diff:
```python
import jax
import jax.numpy as jnp
from jax import lax
from jax.experimental import pallas as pl
from jax.experimental.pallas import tpu as pltpu
from jax.sharding import PartitionSpec as P

HEADS = 128
GROUPS = 8
T = 128
GW = 1280
XW = 1024
CH = 10240
HP = 8192
LOG2E = 1.4426950408889634
EPS = 1e-05
NEG = -1e30
SPAN = 120.0
TINY = 1e-30
MESH = pl.DeviceIdType.MESH
VMEM = pltpu.VMEM

f32 = jnp.float32
bf16 = jnp.bfloat16
NN = ((1,), (0,))
NT = ((1,), (1,))
TN = ((0,), (0,))


def mm(a, b, dims=NN, precision=None):
    return lax.dot_general(a, b, (dims, ((), ())), preferred_element_type=f32, precision=precision)


def iota(shape, dim):
    return lax.broadcasted_iota(jnp.int32, shape, dim)


def sigmoid(v):
    return 0.5 * jnp.tanh(0.5 * v) + 0.5


def split(v):
    hi = v.astype(bf16)
    return hi, (v - hi.astype(f32)).astype(bf16)


def selector(g):
    return (iota((HEADS, XW), 0) == 16 * g + iota((HEADS, XW), 1) // 64).astype(f32).astype(bf16)


def twice(sel):
    return jnp.concatenate([sel, sel], axis=0)


def head_sums(v, sel):
    hi, lo = split(v)
    return mm(hi, sel, NT) + mm(lo, sel, NT)


def place():
    return lax.axis_index("ctx") * 4 + lax.axis_index("head")


def at(p):
    return {"ctx": p // 4, "head": lax.rem(p, 4)}


def off(index, width):
    return pl.multiple_of(index * width, width)


def greet(me):
    barrier = pltpu.get_barrier_semaphore()

    def one(k, carry):
        pl.semaphore_signal(
            barrier, inc=1, device_id=at(lax.rem(me + k, 64)), device_id_type=MESH
        )
        return carry

    lax.fori_loop(1, 64, one, 0)
    return barrier


def await_bytes(ref, sem):
    pltpu.make_async_copy(ref, ref, sem).wait()


def send_slot(me, p, src, dst, send_sem, recv_sem):
    @pl.when(p == me)
    def _():
        pltpu.make_async_copy(src, dst, recv_sem).start()

    @pl.when(p != me)
    def _():
        pltpu.make_async_remote_copy(
            src_ref=src, dst_ref=dst, send_sem=send_sem, recv_sem=recv_sem,
            device_id=at(p), device_id_type=MESH,
        ).start()


def turn(me, i):
    return lax.rem(me // 8 + i, 8)


def load_ext(g, ext, xbc_ref, halo):
    ext[8:136, :] = xbc_ref[:, pl.ds(off(g, GW), GW)].astype(f32)
    rows = pl.multiple_of(g * 32, 32)
    for k in range(3):
        for c in range(10):
            ext[5 + k : 6 + k, 128 * c : 128 * c + 128] = halo[pl.ds(rows + 10 * k + c, 1), :]


def windows(ext, prep_ref, lanes):
    return [
        ext[5:133, lanes] * prep_ref[6],
        ext[6:134, lanes] * prep_ref[7],
        ext[7:135, lanes] * prep_ref[8],
        ext[8:136, lanes],
    ]


def taps_of(w_ref, g, c):
    lanes = pl.ds(pl.multiple_of(lax.rem(g, 2) * GW + 128 * c, 128), 128)
    return [w_ref[g // 2, k : k + 1, lanes] for k in range(5)]


def conv(wins, taps):
    pre = taps[4] + taps[3] * wins[3]
    for k in range(3):
        pre = pre + taps[k] * wins[k]
    return pre


def params(w_ref, row):
    first = 2048 + 32 * row
    return jnp.concatenate([w_ref[q, 5:6, first : first + 32] for q in range(4)], axis=1)


def make_prep(halo, w_ref, dt_ref, seg_ref, prep_ref, pb_ref, segs):
    rate = jnp.exp(params(w_ref, 0))
    dtb = dt_ref[...].astype(f32) + params(w_ref, 1)
    step = jnp.maximum(dtb, 0.0) + jnp.log1p(jnp.exp(-jnp.abs(dtb)))
    decay = -step * rate
    rows, cols = iota((T, T), 0), iota((T, T), 1)
    low = (rows >= cols).astype(f32)
    run = mm(low, decay, NN, lax.Precision.HIGHEST) * LOG2E
    less = run - jnp.log(step) * LOG2E
    seg_row = jnp.broadcast_to(seg_ref[...].astype(f32) + 1.0, (T, T))
    seg_col = seg_row.T
    segs[8:136, :] = seg_col
    segs[5:8, :] = halo[256:259, :]
    prep_ref[0] = run
    prep_ref[1] = less
    prep_ref[2] = run.T
    prep_ref[3] = less.T
    same = seg_col == seg_row
    prep_ref[4] = jnp.where(same & (rows >= cols), 0.0, NEG)
    prep_ref[5] = jnp.where(same & (rows <= cols), 0.0, NEG)
    for k in range(3):
        prep_ref[6 + k] = (segs[5 + k : 133 + k, :] == seg_col).astype(f32)
    prep_ref[9] = step
    prep_ref[10] = decay
    linked = (seg_col == segs[7:8, :]).astype(f32)
    alpha = jnp.exp2(run) * linked
    omega = jnp.exp2(run[T - 1 :] - run) * (seg_col == seg_col[T - 1 :]).astype(f32) * step
    keep = alpha[T - 1 :]
    prep_ref[11] = sigmoid(dtb)
    for i, v in enumerate((alpha, omega)):
        hi, lo = split(v)
        pb_ref[i, :, :T] = hi
        pb_ref[i, :, T:] = lo
    both = jnp.where(rows == 0, params(w_ref, 2), keep)
    hi, lo = split(both)
    pb_ref[2, :, :T] = hi
    pb_ref[2, :, T:] = lo


def conv_group(g, xbc_ref, halo, w_ref, prep_ref, pb_ref, act_ref, pay_ref, ext):
    load_ext(g, ext, xbc_ref, halo)
    base = off(g, GW)
    for c in range(GW // 128):
        pre = conv(windows(ext, prep_ref, slice(128 * c, 128 * c + 128)), taps_of(w_ref, g, c))
        act_ref[:, pl.ds(base + 128 * c, 128)] = (pre * sigmoid(pre)).astype(bf16)
    sel = selector(g)
    omega = mm(pb_ref[1], twice(sel))
    x_ref, b_ref, _ = parts_of(act_ref, g)
    weighted = (omega * x_ref[...].astype(f32)).astype(bf16)
    state = mm(b_ref[...], weighted, TN).astype(bf16)
    khi = mm(pb_ref[2, :16, :T], sel)
    klo = mm(pb_ref[2, :16, T:], sel)
    tail = jnp.where(iota((16, XW), 0) == 0, khi[1:2], klo[1:2]).astype(bf16)
    for i in range(8):
        lanes = slice(128 * i, 128 * i + 128)
        pay_ref[8 * g + i, :128, :] = state[:, lanes]
        pay_ref[8 * g + i, 128:, :] = tail[:, lanes]


def parts_of(act_ref, g):
    base = off(g, GW)
    return (
        act_ref.at[:, pl.ds(base, XW)],
        act_ref.at[:, pl.ds(base + XW, 128)],
        act_ref.at[:, pl.ds(base + XW + 128, 128)],
    )


def halves(v):
    left = iota(v.shape, 1) < 64
    zero = jnp.zeros_like(v)
    return jnp.concatenate([jnp.where(left, v, zero), jnp.where(left, zero, v)], axis=0)


def scan_up(got_ref, start_ref):
    def one(j, state):
        top = jnp.maximum(jnp.max(jnp.abs(state), axis=0, keepdims=True) * 1.01, TINY)
        scale = top.astype(bf16).astype(f32)
        start_ref[j, :128, :] = jnp.exp2(state * (SPAN / scale)).astype(bf16)
        start_ref[j, 128:, :] = jnp.broadcast_to(scale, (16, 128)).astype(bf16)
        tail = got_ref[j, 128:, :].astype(f32)
        keep = tail[0:1] + tail[1:2]
        return keep * state + got_ref[j, :128, :].astype(f32)

    lax.fori_loop(0, 64, one, jnp.zeros((128, 128), f32))


def scan_down(tails_ref, got_ref, end_ref):
    def one(i, grad):
        j = 63 - i
        end_ref[j] = grad.astype(bf16)
        tail = tails_ref[j].astype(f32)
        keep = tail[0:1] + tail[1:2]
        return keep * grad + got_ref[j].astype(f32)

    lax.fori_loop(0, 64, one, jnp.zeros((128, 128), f32))


def wide(slots_ref, g):
    return jnp.concatenate([slots_ref[8 * g + i, :128, :] for i in range(8)], axis=1)


def first_kernel(
    xbc_ref, own_ref, dt_ref, seg_ref,
    act_ref, pay_ref, prep_ref, pb_ref, w_ref, halo, start_ref, tails_ref,
    got, rim, ext, segs, near_send, w_sem, halo_sem, send_sem, recv_sem,
):
    me = place()
    h = lax.axis_index("head")
    barrier = greet(me)

    def pack(c, carry):
        last = xbc_ref[112:128, pl.ds(off(c, 128), 128)].astype(f32)
        for k in range(3):
            rim[pl.ds((c // 10) * 32 + 10 * k + lax.rem(c, 10), 1), :] = last[13 + k : 14 + k]
        return carry

    lax.fori_loop(0, 80, pack, 0)
    for i in range(8):
        rim[32 * i + 30 : 32 * i + 32, :] = jnp.zeros((2, 128), f32)
    ids = jnp.broadcast_to(seg_ref[...].astype(f32) + 1.0, (T, T)).T
    rim[256:264, :] = jnp.zeros((8, 128), f32)
    rim[256:259, :] = ids[T - 3 :]
    pl.semaphore_wait(barrier, 63)

    pltpu.make_async_copy(own_ref, w_ref.at[h], w_sem).start()
    for k in range(1, 4):
        pltpu.make_async_remote_copy(
            src_ref=own_ref, dst_ref=w_ref.at[h], send_sem=near_send, recv_sem=w_sem,
            device_id=at(me - h + lax.rem(h + k, 4)), device_id_type=MESH,
        ).start()

    @pl.when(me < 63)
    def _():
        pltpu.make_async_remote_copy(
            src_ref=rim, dst_ref=halo, send_sem=send_sem, recv_sem=halo_sem,
            device_id=at(lax.rem(me + 1, 64)), device_id_type=MESH,
        ).start()

    @pl.when(me == 0)
    def _():
        halo[...] = jnp.zeros_like(halo)

    await_bytes(w_ref, w_sem)
    await_bytes(w_ref.at[pl.ds(0, 3)], near_send)

    @pl.when(me > 0)
    def _():
        await_bytes(halo, halo_sem)

    @pl.when(me < 63)
    def _():
        await_bytes(rim, send_sem)

    make_prep(halo, w_ref, dt_ref, seg_ref, prep_ref, pb_ref, segs)

    def one(i, carry):
        g = turn(me, i)
        conv_group(g, xbc_ref, halo, w_ref, prep_ref, pb_ref, act_ref, pay_ref, ext)
        for s in range(8):
            p = 8 * g + s
            send_slot(me, p, pay_ref.at[p], got.at[me], send_sem, recv_sem)
        return carry

    lax.fori_loop(0, 8, one, 0)
    await_bytes(got, recv_sem)
    scan_up(got, start_ref)
    tails_ref[...] = got[:, 128:, :]
    await_bytes(got.at[pl.ds(0, 63)], send_sem)


def inner_forward(g, act_ref, prep_ref, y_ref):
    x_ref, b_ref, c_ref = parts_of(act_ref, g)
    scores = mm(c_ref[...], b_ref[...], NT)
    run = pltpu.roll(prep_ref[0], lax.rem(128 - 16 * g, 128), 1)
    less = prep_ref[3, pl.ds(off(g, 16), 16), :]
    bias = prep_ref[4]
    for pair in range(8):
        mats = []
        for j in (2 * pair, 2 * pair + 1):
            el = jnp.exp2(run[:, j : j + 1] - less[j : j + 1, :] + bias)
            mats.append((el * scores).astype(bf16))
        lanes = slice(128 * pair, 128 * pair + 128)
        y_ref[:, pl.ds(off(g, XW) + 128 * pair, 128)] = mm(
            jnp.concatenate(mats, axis=1), halves(x_ref[:, lanes])
        )


def decode(code_ref, g):
    codes = wide(code_ref, g).astype(f32)
    scale = jnp.concatenate([code_ref[8 * g + i, 128:, :] for i in range(8)], axis=1)
    return jnp.log2(codes) * (scale[0:1].astype(f32) * (1.0 / SPAN))


def gate_group(
    g, act_ref, yi_ref, code_ref, start_ref, gate_ref, cot_ref, w_ref, pb_ref,
    dy_ref, dgate_ref, pay_ref, dcc_ref, rsum_ref, dgain_ref, dskip_ref,
    alpha_s, cs_s, ady_s, qhi_s, qlo_s,
):
    x_ref, _, c_ref = parts_of(act_ref, g)
    base = pl.ds(off(g, XW), XW)
    yi_ref, gate_ref, cot_ref = yi_ref.at[:, base], gate_ref.at[:, base], cot_ref.at[:, base]
    dy_ref, dgate_ref = dy_ref.at[:, base], dgate_ref.at[:, base]
    sel = selector(g)
    both = twice(sel)
    start, start_lo = split(decode(code_ref, g))
    for i in range(8):
        start_ref[8 * g + i] = start[:, 128 * i : 128 * i + 128]
    cs_s[...] = mm(c_ref[...], start) + mm(c_ref[...], start_lo)
    alpha_s[...] = mm(pb_ref[0], both)
    skip = mm(pb_ref[2, :16, :], both)[0:1]
    gain = w_ref[g // 2, 5:6, pl.ds(off(lax.rem(g, 2), XW), XW)]
    dgain = jnp.zeros((16, XW), f32)
    dskip = jnp.zeros((16, XW), f32)
    for r in range(8):
        rows = slice(16 * r, 16 * r + 16)
        alpha = alpha_s[rows, :]
        yssm = yi_ref[rows, :] + alpha * cs_s[rows, :]
        x = x_ref[rows, :].astype(f32)
        ssm = (yssm + skip * x).astype(bf16).astype(f32)
        gate = gate_ref[rows, :].astype(f32)
        sg = sigmoid(gate)
        sl = gate * sg
        gated = ssm * sl
        rr = lax.rsqrt(jnp.sum(gated * gated, axis=1, keepdims=True) * (1.0 / XW) + EPS)
        norm = gated * rr
        cot = cot_ref[rows, :].astype(f32)
        dgain = dgain + cot * norm
        dn = cot * gain
        m2 = jnp.sum(dn * norm, axis=1, keepdims=True) * (1.0 / XW)
        dgated = rr * (dn - norm * m2)
        dy = (dgated * sl).astype(bf16)
        dy_ref[rows, :] = dy
        dgate_ref[rows, :] = (dgated * ssm * (sg + sl * (1.0 - sg))).astype(bf16)
        dyf = dy.astype(f32)
        ady_s[rows, :] = (alpha * dyf).astype(bf16)
        hi, lo = split(dyf * yssm)
        qhi_s[rows, :] = hi
        qlo_s[rows, :] = lo
        dskip = dskip + dyf * x
    ady = ady_s[...]
    dstart = mm(c_ref[...], ady, TN).astype(bf16)
    for i in range(8):
        pay_ref[8 * g + i] = dstart[:, 128 * i : 128 * i + 128]
    dcc_ref[g] = mm(ady, start, NT) + mm(ady, start_lo, NT)
    rsum_ref[...] += mm(qhi_s[...], sel, NT) + mm(qlo_s[...], sel, NT)
    dskip_ref[...] += head_sums(dskip, sel)
    dgain_ref[g] = jnp.sum(dgain, axis=0, keepdims=True)


def send_back(me, values, landing, send_sem, recv_sems):
    mine = me // 8

    def one(i, carry):
        group = lax.rem(mine + 8 - i, 8)
        for s in range(8):
            p = 8 * group + s
            send_slot(me, p, values.at[p], landing.at[me], send_sem, recv_sems.at[mine])
        return carry

    lax.fori_loop(0, 8, one, 0)


def second_kernel(
    act_ref, start_own, tails_ref, gate_ref, cot_ref, w_ref, prep_ref, pb_ref,
    start_ref, dy_ref, dgate_ref, dcc_ref, rsum_ref, dgain_ref, dskip_ref, end_ref,
    codes, yi_s, pay, got, alpha_s, cs_s, ady_s, qhi_s, qlo_s, back_send, back_recv, send_sem, recv_sem,
):
    me = place()
    barrier = greet(me)
    rsum_ref[...] = jnp.zeros_like(rsum_ref)
    dskip_ref[...] = jnp.zeros_like(dskip_ref)

    def forward(i, carry):
        inner_forward(i, act_ref, prep_ref, yi_s)
        return carry

    lax.fori_loop(0, 8, forward, 0)
    pl.semaphore_wait(barrier, 63)
    send_back(me, start_own, codes, back_send, back_recv)

    def one(i, carry):
        g = turn(me, i)
        await_bytes(codes.at[pl.ds(8 * g, 8)], back_recv.at[g])
        gate_group(
            g, act_ref, yi_s, codes, start_ref, gate_ref, cot_ref, w_ref, pb_ref,
            dy_ref, dgate_ref, pay, dcc_ref, rsum_ref, dgain_ref, dskip_ref,
            alpha_s, cs_s, ady_s, qhi_s, qlo_s,
        )
        for s in range(8):
            p = 8 * g + s
            send_slot(me, p, pay.at[p], got.at[me], send_sem, recv_sem)
        return carry

    lax.fori_loop(0, 8, one, 0)
    await_bytes(got, recv_sem)
    scan_down(tails_ref, got, end_ref)
    await_bytes(got.at[pl.ds(0, 63)], send_sem)
    await_bytes(codes.at[pl.ds(0, 63)], back_send)


def inner_backward(g, act_ref, dy_ref, prep_ref, dcc_ref, dx_ref, db_ref, dc_ref):
    x_ref, b_ref, c_ref = parts_of(act_ref, g)
    scores = mm(b_ref[...], c_ref[...], NT)
    less = pltpu.roll(prep_ref[1], lax.rem(128 - 16 * g, 128), 1)
    run = prep_ref[2, pl.ds(off(g, 16), 16), :]
    bias = prep_ref[5]
    dscores = jnp.zeros((T, T), f32)
    for pair in range(8):
        out_lanes = pl.ds(off(g, XW) + 128 * pair, 128)
        dy2 = halves(dy_ref[:, out_lanes])
        dmat = mm(x_ref[:, 128 * pair : 128 * pair + 128], dy2, NT)
        mats = []
        for i in range(2):
            j = 2 * pair + i
            el = jnp.exp2(run[j : j + 1, :] - less[:, j : j + 1] + bias)
            mats.append((el * scores).astype(bf16))
            dscores = dscores + el * dmat[:, 128 * i : 128 * i + 128]
        dx_ref[:, out_lanes] = mm(jnp.concatenate(mats, axis=1), dy2)
    ds = dscores.astype(bf16)
    db_ref[g] = mm(ds, c_ref[...])
    dc_ref[g] = dcc_ref[g] + mm(ds, b_ref[...], TN)


def back_group(
    g, xbc_ref, halo, w_ref, act_ref, dy_ref, dxi, dbi, dci, start_ref, pay_ref, end,
    prep_ref, pb_ref, dgain_ref, dxbc_ref, tail, rim, part, ext, dact, csum, ksum,
):
    x_ref, b_ref, _ = parts_of(act_ref, g)
    base = pl.ds(off(g, XW), XW)
    sel = selector(g)
    both = twice(sel)
    end_g = wide(end, g)
    rows16 = mm(pb_ref[2, :16, :], both)
    skip, keep = rows16[0:1], rows16[1:2]
    omega = mm(pb_ref[1], both)
    x = x_ref[...].astype(f32)
    dxs = dxi[:, base] + omega * mm(b_ref[...], end_g)
    csum[...] += head_sums(x * dxs, sel)
    dact[:, :XW] = (dxs + skip * dy_ref[:, base].astype(f32)).astype(bf16)
    dact[:, XW : XW + 128] = (dbi[g] + mm((omega * x).astype(bf16), end_g, NT)).astype(bf16)
    dact[:, XW + 128 :] = dci[g].astype(bf16)
    final = keep * wide(start_ref, g).astype(f32) + wide(pay_ref, g).astype(f32)
    ksum[...] += head_sums(jnp.sum((final * end_g.astype(f32)).reshape(16, 8, XW), axis=0), sel)

    load_ext(g, ext, xbc_ref, halo)
    rows = iota((T, 128), 0)
    for c in range(GW // 128):
        lanes = slice(128 * c, 128 * c + 128)
        wide_lanes = pl.ds(off(g, GW) + 128 * c, 128)
        wins = windows(ext, prep_ref, lanes)
        taps = taps_of(w_ref, g, c)
        pre = conv(wins, taps)
        sg = sigmoid(pre)
        dpre = dact[:, lanes].astype(f32) * (sg + pre * sg * (1.0 - sg))
        for k in range(4):
            part[g, c, k : k + 1, :] = jnp.sum(dpre * wins[k], axis=0, keepdims=True)
        part[g, c, 4:5, :] = jnp.sum(dpre, axis=0, keepdims=True)
        if c < 8:
            part[g, c, 5:6, :] = dgain_ref[g, :, lanes]
        else:
            part[g, c, 5:6, :] = jnp.zeros((1, 128), f32)
        part[g, c, 6:8, :] = jnp.zeros((2, 128), f32)
        total = taps[3] * dpre
        over = jnp.zeros((8, 128), f32)
        for k in range(3):
            far = 3 - k
            moved = pltpu.roll(taps[k] * dpre * prep_ref[6 + k], T - far, 0)
            inside = rows < T - far
            total = total + jnp.where(inside, moved, 0.0)
            over = over + jnp.where(inside, 0.0, moved)[T - 8 :]
        dxbc_ref[:, wide_lanes] = total.astype(bf16)
        tail[:, wide_lanes] = total[T - 16 :]
        for k in range(3):
            rim[pl.ds(pl.multiple_of(g * 32, 32) + 10 * k + c, 1), :] = over[5 + k : 6 + k]


def third_kernel(
    xbc_ref, halo, w_ref, act_ref, dy_ref, dcc_ref, start_ref, pay_ref, end_own,
    prep_ref, pb_ref, rsum_ref, dgain_ref, dskip_ref,
    dxbc_ref, ddt_ref, gconv_ref, ggain_ref, gheads_ref,
    dxi, dbi, dci, end, tail, rim, rim_in, part, ext, dact, csum, ksum,
    zbuf, hbuf, own, dhead, rbuf, total, fbuf,
    back_send, back_recv, rim_send, rim_sem, z_send, z_sem, h_send, h_sem,
    r_send, r_sem, f_send, f_sem,
):
    me = place()
    c, h, d = lax.axis_index("ctx"), lax.axis_index("head"), lax.axis_index("dp")
    barrier = greet(me)

    def greet_twin(k, carry):
        pl.semaphore_signal(
            barrier, inc=1, device_id={"dp": 1 - d, "ctx": k, "head": h}, device_id_type=MESH
        )
        return carry

    lax.fori_loop(0, 16, greet_twin, 0)
    csum[...] = jnp.zeros_like(csum)
    ksum[...] = jnp.zeros_like(ksum)
    rim[...] = jnp.zeros_like(rim)

    def inner(i, carry):
        inner_backward(i, act_ref, dy_ref, prep_ref, dcc_ref, dxi, dbi, dci)
        return carry

    lax.fori_loop(0, 8, inner, 0)
    pl.semaphore_wait(barrier, 63 + 16)
    send_back(me, end_own, end, back_send, back_recv)

    def one(i, carry):
        g = turn(me, i)
        await_bytes(end.at[pl.ds(8 * g, 8)], back_recv.at[g])
        back_group(
            g, xbc_ref, halo, w_ref, act_ref, dy_ref, dxi, dbi, dci, start_ref, pay_ref, end,
            prep_ref, pb_ref, dgain_ref, dxbc_ref, tail, rim, part, ext, dact, csum, ksum,
        )
        send_slot(
            me, me - h + g // 2, part.at[g], zbuf.at[h, lax.rem(g, 2)], z_send, z_sem
        )

        @pl.when(me > 0)
        def _():
            rows = pl.ds(pl.multiple_of(g * 32, 32), 32)
            pltpu.make_async_remote_copy(
                src_ref=rim.at[rows], dst_ref=rim_in.at[rows], send_sem=rim_send,
                recv_sem=rim_sem, device_id=at(lax.rem(me + 63, 64)), device_id_type=MESH,
            ).start()

        return carry

    lax.fori_loop(0, 8, one, 0)

    high = (iota((T, T), 0) <= iota((T, T), 1)).astype(f32)
    step, decay = prep_ref[9], prep_ref[10]
    col = csum[...]
    dlog = mm(high, rsum_ref[...] - col, NN, lax.Precision.HIGHEST)
    dlog = dlog + jnp.sum(ksum[...], axis=0, keepdims=True)
    dstep = col / step - dlog * jnp.exp(params(w_ref, 0))
    ddt = dstep * prep_ref[11]
    ddt_ref[...] = ddt.astype(bf16)
    dhead[0:1, :] = jnp.sum(dlog * decay, axis=0, keepdims=True)
    dhead[1:2, :] = jnp.sum(ddt, axis=0, keepdims=True)
    dhead[2:3, :] = jnp.sum(dskip_ref[...], axis=0, keepdims=True)
    dhead[3:8, :] = jnp.zeros((5, HEADS), f32)
    pltpu.make_async_copy(dhead, hbuf.at[h], h_sem).start()
    for k in range(1, 4):
        pltpu.make_async_remote_copy(
            src_ref=dhead, dst_ref=hbuf.at[h], send_sem=h_send, recv_sem=h_sem,
            device_id=at(me - h + lax.rem(h + k, 4)), device_id_type=MESH,
        ).start()

    await_bytes(zbuf, z_sem)
    for q in range(2):
        own[10 * q : 10 * q + 10] = zbuf[0, q] + zbuf[1, q] + zbuf[2, q] + zbuf[3, q]
    await_bytes(hbuf, h_sem)
    own[20] = hbuf[0] + hbuf[1] + hbuf[2] + hbuf[3]
    rank = d * 16 + c

    def to_rank(r, src, dst, send_sem, recv_sem):
        @pl.when(r == rank)
        def _():
            pltpu.make_async_copy(src, dst, recv_sem).start()

        @pl.when(r != rank)
        def _():
            pltpu.make_async_remote_copy(
                src_ref=src, dst_ref=dst, send_sem=send_sem, recv_sem=recv_sem,
                device_id={"dp": r // 16, "ctx": lax.rem(r, 16), "head": h},
                device_id_type=MESH,
            ).start()

    def spread(r, carry):
        to_rank(r, own.at[r], rbuf.at[rank], r_send, r_sem)
        return carry

    lax.fori_loop(0, 21, spread, 0)

    @pl.when(rank < 21)
    def _():
        await_bytes(rbuf, r_sem)
        total[...] = jnp.sum(rbuf[...], axis=0)

        def share(k, carry):
            to_rank(lax.rem(rank + k, 32), total, fbuf.at[rank], f_send, f_sem)
            return carry

        lax.fori_loop(0, 32, share, 0)

    @pl.when(me < 63)
    def _():
        await_bytes(rim_in, rim_sem)

        def fix(t, carry):
            lanes = pl.ds(off(t, 128), 128)
            for k in range(3):
                row = rim_in[pl.ds((t // 10) * 32 + 10 * k + lax.rem(t, 10), 1), :]
                tail[13 + k : 14 + k, lanes] += row
            dxbc_ref[112:128, lanes] = tail[:, lanes].astype(bf16)
            return carry

        lax.fori_loop(0, 80, fix, 0)

    await_bytes(fbuf, f_sem)
    for q in range(2):
        for t in range(10):
            lanes = slice(GW * q + 128 * t, GW * q + 128 * t + 128)
            gconv_ref[:, lanes] = fbuf[10 * q + t, :5, :]
            if t < 8:
                lanes = slice(XW * q + 128 * t, XW * q + 128 * t + 128)
                ggain_ref[:, lanes] = fbuf[10 * q + t, 5:6, :]
    gheads_ref[...] = pltpu.roll(fbuf[20], lax.rem(128 - 32 * h, 128), 1)[:3, :32]

    await_bytes(end.at[pl.ds(0, 63)], back_send)
    await_bytes(hbuf.at[pl.ds(0, 3)], h_send)
    await_bytes(part.at[pl.ds(0, 6)], z_send)

    @pl.when(me > 0)
    def _():
        await_bytes(rim, rim_send)

    @pl.when(rank < 21)
    def _():
        await_bytes(rbuf.at[pl.ds(0, 20)], r_send)
        await_bytes(rbuf.at[pl.ds(0, 31)], f_send)

    @pl.when(rank >= 21)
    def _():
        await_bytes(rbuf.at[pl.ds(0, 21)], r_send)


def S(shape, dtype):
    return jax.ShapeDtypeStruct(shape, dtype)


def call(kernel, name, ins, outs, scratch, cid):
    spec = pl.BlockSpec(memory_space=VMEM)
    return pl.pallas_call(
        kernel,
        in_specs=[spec] * len(ins),
        out_specs=[spec] * len(outs),
        out_shape=outs,
        scratch_shapes=scratch,
        compiler_params=pltpu.CompilerParams(
            vmem_limit_bytes=56 << 20, collective_id=cid, has_side_effects=True
        ),
        cost_estimate=pl.CostEstimate(flops=4 << 30, bytes_accessed=16 << 20, transcendentals=0),
        name=name,
    )(*ins)


def body(
    xbc_raw, gate_raw, dt_raw, segment_ids, conv_weight, norm_gain, head_params, out_cotangent
):
    xbc, gate, dt, cot = xbc_raw[0], gate_raw[0], dt_raw[0], out_cotangent[0]
    own_w = jnp.concatenate(
        [
            conv_weight,
            jnp.concatenate(
                [norm_gain[None], head_params.reshape(1, 96), jnp.zeros((1, 416), f32)], axis=1
            ),
        ],
        axis=0,
    )
    dma = pltpu.SemaphoreType.DMA
    act, pay, prep, pb, w_all, halo, starts, tails = call(
        first_kernel,
        "conv_states",
        (xbc, own_w, dt, segment_ids),
        (
            S((T, CH), bf16),
            S((64, 144, 128), bf16),
            S((12, T, T), f32),
            S((3, T, 2 * T), bf16),
            S((4, 6, 2560), f32),
            S((264, 128), f32),
            S((64, 144, 128), bf16),
            S((64, 16, 128), bf16),
        ),
        (
            VMEM((64, 144, 128), bf16),
            VMEM((264, 128), f32),
            VMEM((136, GW), f32),
            VMEM((136, 128), f32),
            dma, dma, dma, dma, dma,
        ),
        1,
    )
    start, dy, dgate, dcc, rsum, dgain, dskip, ends = call(
        second_kernel,
        "gate_norm",
        (act, starts, tails, gate, cot, w_all, prep, pb),
        (
            S((64, 128, 128), bf16),
            S((T, HP), bf16),
            S((T, HP), bf16),
            S((8, T, 128), f32),
            S((T, HEADS), f32),
            S((8, 1, XW), f32),
            S((16, HEADS), f32),
            S((64, 128, 128), bf16),
        ),
        (
            VMEM((64, 144, 128), bf16),
            VMEM((T, HP), f32),
            VMEM((64, 128, 128), bf16),
            VMEM((64, 128, 128), bf16),
            VMEM((T, XW), f32),
            VMEM((T, XW), f32),
            VMEM((T, XW), bf16),
            VMEM((T, XW), bf16),
            VMEM((T, XW), bf16),
            dma, dma((8,)), dma, dma,
        ),
        2,
    )
    dxbc, ddt, gconv, ggain, gheads = call(
        third_kernel,
        "conv_backward",
        (xbc, halo, w_all, act, dy, dcc, start, pay, ends, prep, pb, rsum, dgain, dskip),
        (
            S((T, CH), bf16),
            S((T, HEADS), bf16),
            S((5, 2560), f32),
            S((1, 2048), f32),
            S((3, 32), f32),
        ),
        (
            VMEM((T, HP), f32),
            VMEM((8, T, 128), f32),
            VMEM((8, T, 128), f32),
            VMEM((64, 128, 128), bf16),
            VMEM((16, CH), f32),
            VMEM((256, 128), f32),
            VMEM((256, 128), f32),
            VMEM((8, 10, 8, 128), f32),
            VMEM((136, GW), f32),
            VMEM((T, GW), bf16),
            VMEM((T, HEADS), f32),
            VMEM((8, HEADS), f32),
            VMEM((4, 2, 10, 8, 128), f32),
            VMEM((4, 8, 128), f32),
            VMEM((21, 8, 128), f32),
            VMEM((8, 128), f32),
            VMEM((32, 8, 128), f32),
            VMEM((8, 128), f32),
            VMEM((21, 8, 128), f32),
            dma, dma((8,)), dma, dma, dma, dma, dma, dma, dma, dma, dma, dma,
        ),
        3,
    )
    return (dxbc[None], dgate[None], ddt[None], gconv, ggain[0], gheads)


def solution(mesh):
    token = P("dp", ("ctx", "head"), None)
    return jax.shard_map(
        body,
        mesh=mesh,
        in_specs=(
            token, token, token, P("dp", ("ctx", "head")),
            P(None, "head"), P("head"), P(None, "head"), token,
        ),
        out_specs=(token, token, token, P(None, "head"), P("head"), P(None, "head")),
        check_vma=False,
    )
```

time: 256 us -> 218 us (0.85)
  Pallas kernels: 68.2 us -> 207 us
  blocking collectives: 73.1 us -> 0 us
  waiting for transfers between devices: 46.7 us -> 0 us
  starting transfers between devices: 35.7 us -> 0 us
  local copies, waits for them, and re-layouts: 28 us -> 8.94 us
    pallas_call x7 -> x3, Pallas kernels: 68.2 us -> 207 us  [call(): pl.pallas_call(kernel, in_specs=[spec] * len(ins), out_specs=[spec] * len...]
    all_to_all x2 -> x0, blocking collectives: 73.1 us -> none  [the longest x1 40.8 us: body(): got = lax.all_to_all(pay, along, split_axis=0, concat_axis=0, tiled=True)]
    all_to_all x5 -> x0, waiting for transfers between devices: 45.3 us -> none  [the longest x1 17.8 us: body(): lax.all_to_all(starts, along, split_axis=0, concat_axis=0, tiled=True)]
    all_to_all x5 -> x0, starting transfers between devices: 31 us -> none  [the longest x1 8.36 us: body(): lax.all_to_all(pieces, everyone, split_axis=0, concat_axis=0, tiled=True)]
    unnamed x43 -> x16, local copies, waits for them, and re-layouts: 17.7 us -> 7.38 us
    ppermute x2 -> x0, starting transfers between devices: 4.66 us -> none  [the longest x1 3.37 us: body(): lax.ppermute(jnp.concatenate([xbc[T - 3:], last_ids], axis=1), along, up)]
    slice x7 -> x0, local copies, waits for them, and re-layouts: 3.28 us -> none  [the longest x1 1.01 us: body(): rim_in = lax.ppermute(rim[5:].astype(bf16), along, down)]
  transfers between devices with their start and end apart: 7 -> 0, of which waited for: 5 -> 0; matrix products, arithmetic and copies ran while one was open for 2% -> 0% of each run, Pallas kernels for 6% -> 0%
where the time goes in v2:
time: 218 us
  Pallas kernels  207 us (95%)
  local copies, waits for them, and re-layouts  8.94 us (4%)
    pallas_call x3, Pallas kernels, call(): pl.pallas_call(kernel, in_specs=[spec] * len(ins), out_specs=[spec] * len...  207 us
    unnamed x16, local copies, waits for them, and re-layouts  7.38 us

profile of v2, /device:TPU:1, one launch (start us, length us, event | category | flops | bytes accessed | tf_op | source)
XLA Modules:
  0.0 217.8 jit_solution(8967244167096625642)
XLA Ops:
  0.6 0.8 reshape.15
  1.4 0.8 concatenate.6
  2.2 1.5 pad_maximum_fusion.own_ref
  3.7 58.8 %conv_states.1 = (bf16[128,10240]{1,0:T(8,128)(2,1)}, bf16[64,144,128]{2,1,0:T(8,128)(2,1)}, f32[12,128,128]{2,1,0:T(8,128)}, bf16[3,128,256]{2,1,0:T(8,128)(2,1...) custom-call(bf16[128,10240]{1,0:T(8,128)(2,1)} %bitcast.9, ...), custom_call_target="tpu_custom_call" | custom-call | flops 4294967296 | bytes 16777216 | tf_op jit(solution)/shard_map/conv_states/pallas_call | solution.py:676
  62.6 75.9 %gate_norm.1 = (bf16[64,128,128]{2,1,0:T(8,128)(2,1)}, bf16[128,8192]{1,0:T(8,128)(2,1)}, bf16[128,8192]{1,0:T(8,128)(2,1)}, f32[8,128,128]{2,1,0:T(8,128)}, f32...) custom-call(bf16[128,10240]{1,0:T(8,128)(2,1)} %get-tuple-element.29.act_ref, ...), custom_call_target="tpu_custom_call" | custom-call | flops 4294967296 | bytes 16777216 | tf_op jit(solution)/shard_map/gate_norm/pallas_call | solution.py:676
  138.5 72.0 %conv_backward.1 = (bf16[128,10240]{1,0:T(8,128)(2,1)}, bf16[128,128]{1,0:T(8,128)(2,1)}, f32[5,2560]{1,0:T(8,128)}, f32[1,2048]{1,0:T(1,128)}, f32[3,32]{1,0:T(4,128)}) custom-call(bf16[128,10240]{1,0:T(8,128)(2,1)} %bitcast.10, f32[264,128]{1,0:T(8,128)} %get-tuple-element.27.halo, f32[4,6,2560]{2,1,0:T(8,128)} %get-tuple-element.28.w_ref, ...), custom_call_target="tpu_custom_call" | custom-call | flops 4294967296 | bytes 16777216 | tf_op jit(solution)/shard_map/conv_backward/pallas_call | solution.py:676
  210.4 0.0 copy-start
  210.4 3.6 %copy.20 = bf16[1,128,10240]{2,1,0:T(8,128)(2,1)} copy(bf16[1,128,10240]{2,1,0:T(8,128)(2,1)} %bitcast.11) | data formatting | bytes 5242880
  214.1 0.0 copy-done
  214.1 0.0 copy-start.2
  214.1 0.0 copy-start.1
  214.1 0.0 copy-start.3
  214.1 0.0 copy-start.4
  214.1 1.3 copy.21
  215.4 0.0 copy-done.2
  215.4 0.6 copy.22
  216.0 0.0 copy-done.1
  216.0 0.6 copy.23
  216.7 0.0 copy-done.3
  216.7 0.6 copy.24
  217.3 0.0 copy-done.4
  217.3 0.6 copy.25
  (1 shorter events, 0.0 us)
Async XLA Ops:
  210.4 3.6 %copy-start = (bf16[128,8192]{1,0:T(8,128)(2,1)S(1)}, bf16[128,8192]{1,0:T(8,128)(2,1)}, u32[]{:S(2)}) copy-start(bf16[128,8192]{1,0:T(8,128)(2,1)} %get-tuple-element.43) | copy-start | bytes 6291460
  214.1 1.3 copy-start.2
  214.1 2.0 copy-start.1
  214.1 2.6 %copy-start.3 = (f32[1,2048]{1,0:T(1,128)S(1)}, f32[1,2048]{1,0:T(1,128)}, u32[]{:S(2)}) copy-start(f32[1,2048]{1,0:T(1,128)} %get-tuple-element.46) | copy-start | bytes 24580
  214.1 3.2 %copy-start.4 = (f32[3,32]{1,0:T(4,128)S(1)}, f32[3,32]{1,0:T(4,128)}, u32[]{:S(2)}) copy-start(f32[3,32]{1,0:T(4,128)} %get-tuple-element.59) | copy-start | bytes 1156

commit v3 on v2

--- a/solution.py
+++ b/solution.py
@@ -224,11 +224,11 @@
     lax.fori_loop(0, 64, one, jnp.zeros((128, 128), f32))
 
 
-def scan_down(tails_ref, got_ref, end_ref):
+def scan_down(got_up, got_ref, end_ref):
     def one(i, grad):
         j = 63 - i
         end_ref[j] = grad.astype(bf16)
-        tail = tails_ref[j].astype(f32)
+        tail = got_up[j, 128:, :].astype(f32)
         keep = tail[0:1] + tail[1:2]
         return keep * grad + got_ref[j].astype(f32)
 
@@ -237,75 +237,6 @@
 
 def wide(slots_ref, g):
     return jnp.concatenate([slots_ref[8 * g + i, :128, :] for i in range(8)], axis=1)
-
-
-def first_kernel(
-    xbc_ref, own_ref, dt_ref, seg_ref,
-    act_ref, pay_ref, prep_ref, pb_ref, w_ref, halo, start_ref, tails_ref,
-    got, rim, ext, segs, near_send, w_sem, halo_sem, send_sem, recv_sem,
-):
-    me = place()
-    h = lax.axis_index("head")
-    barrier = greet(me)
-
-    def pack(c, carry):
-        last = xbc_ref[112:128, pl.ds(off(c, 128), 128)].astype(f32)
-        for k in range(3):
-            rim[pl.ds((c // 10) * 32 + 10 * k + lax.rem(c, 10), 1), :] = last[13 + k : 14 + k]
-        return carry
-
-    lax.fori_loop(0, 80, pack, 0)
-    for i in range(8):
-        rim[32 * i + 30 : 32 * i + 32, :] = jnp.zeros((2, 128), f32)
-    ids = jnp.broadcast_to(seg_ref[...].astype(f32) + 1.0, (T, T)).T
-    rim[256:264, :] = jnp.zeros((8, 128), f32)
-    rim[256:259, :] = ids[T - 3 :]
-    pl.semaphore_wait(barrier, 63)
-
-    pltpu.make_async_copy(own_ref, w_ref.at[h], w_sem).start()
-    for k in range(1, 4):
-        pltpu.make_async_remote_copy(
-            src_ref=own_ref, dst_ref=w_ref.at[h], send_sem=near_send, recv_sem=w_sem,
-            device_id=at(me - h + lax.rem(h + k, 4)), device_id_type=MESH,
-        ).start()
-
-    @pl.when(me < 63)
-    def _():
-        pltpu.make_async_remote_copy(
-            src_ref=rim, dst_ref=halo, send_sem=send_sem, recv_sem=halo_sem,
-            device_id=at(lax.rem(me + 1, 64)), device_id_type=MESH,
-        ).start()
-
-    @pl.when(me == 0)
-    def _():
-        halo[...] = jnp.zeros_like(halo)
-
-    await_bytes(w_ref, w_sem)
-    await_bytes(w_ref.at[pl.ds(0, 3)], near_send)
-
-    @pl.when(me > 0)
-    def _():
-        await_bytes(halo, halo_sem)
-
-    @pl.when(me < 63)
-    def _():
-        await_bytes(rim, send_sem)
-
-    make_prep(halo, w_ref, dt_ref, seg_ref, prep_ref, pb_ref, segs)
-
-    def one(i, carry):
-        g = turn(me, i)
-        conv_group(g, xbc_ref, halo, w_ref, prep_ref, pb_ref, act_ref, pay_ref, ext)
-        for s in range(8):
-            p = 8 * g + s
-            send_slot(me, p, pay_ref.at[p], got.at[me], send_sem, recv_sem)
-        return carry
-
-    lax.fori_loop(0, 8, one, 0)
-    await_bytes(got, recv_sem)
-    scan_up(got, start_ref)
-    tails_ref[...] = got[:, 128:, :]
-    await_bytes(got.at[pl.ds(0, 63)], send_sem)
 
 
 def inner_forward(g, act_ref, prep_ref, y_ref):
@@ -400,44 +331,6 @@
     lax.fori_loop(0, 8, one, 0)
 
 
-def second_kernel(
-    act_ref, start_own, tails_ref, gate_ref, cot_ref, w_ref, prep_ref, pb_ref,
-    start_ref, dy_ref, dgate_ref, dcc_ref, rsum_ref, dgain_ref, dskip_ref, end_ref,
-    codes, yi_s, pay, got, alpha_s, cs_s, ady_s, qhi_s, qlo_s, back_send, back_recv, send_sem, recv_sem,
-):
-    me = place()
-    barrier = greet(me)
-    rsum_ref[...] = jnp.zeros_like(rsum_ref)
-    dskip_ref[...] = jnp.zeros_like(dskip_ref)
-
-    def forward(i, carry):
-        inner_forward(i, act_ref, prep_ref, yi_s)
-        return carry
-
-    lax.fori_loop(0, 8, forward, 0)
-    pl.semaphore_wait(barrier, 63)
-    send_back(me, start_own, codes, back_send, back_recv)
-
-    def one(i, carry):
-        g = turn(me, i)
-        await_bytes(codes.at[pl.ds(8 * g, 8)], back_recv.at[g])
-        gate_group(
-            g, act_ref, yi_s, codes, start_ref, gate_ref, cot_ref, w_ref, pb_ref,
-            dy_ref, dgate_ref, pay, dcc_ref, rsum_ref, dgain_ref, dskip_ref,
-            alpha_s, cs_s, ady_s, qhi_s, qlo_s,
-        )
-        for s in range(8):
-            p = 8 * g + s
-            send_slot(me, p, pay.at[p], got.at[me], send_sem, recv_sem)
-        return carry
-
-    lax.fori_loop(0, 8, one, 0)
-    await_bytes(got, recv_sem)
-    scan_down(tails_ref, got, end_ref)
-    await_bytes(got.at[pl.ds(0, 63)], send_sem)
-    await_bytes(codes.at[pl.ds(0, 63)], back_send)
-
-
 def inner_backward(g, act_ref, dy_ref, prep_ref, dcc_ref, dx_ref, db_ref, dc_ref):
     x_ref, b_ref, c_ref = parts_of(act_ref, g)
     scores = mm(b_ref[...], c_ref[...], NT)
@@ -514,14 +407,16 @@
             rim[pl.ds(pl.multiple_of(g * 32, 32) + 10 * k + c, 1), :] = over[5 + k : 6 + k]
 
 
-def third_kernel(
-    xbc_ref, halo, w_ref, act_ref, dy_ref, dcc_ref, start_ref, pay_ref, end_own,
-    prep_ref, pb_ref, rsum_ref, dgain_ref, dskip_ref,
-    dxbc_ref, ddt_ref, gconv_ref, ggain_ref, gheads_ref,
-    dxi, dbi, dci, end, tail, rim, rim_in, part, ext, dact, csum, ksum,
-    zbuf, hbuf, own, dhead, rbuf, total, fbuf,
-    back_send, back_recv, rim_send, rim_sem, z_send, z_sem, h_send, h_sem,
-    r_send, r_sem, f_send, f_sem,
+def mixer(
+    xbc_ref, own_ref, dt_ref, seg_ref, gate_hbm, cot_hbm,
+    dxbc_ref, dgate_hbm, ddt_ref, gconv_ref, ggain_ref, gheads_ref,
+    gate_v, cot_v, dgate_v, act_ref, pay_ref, prep_ref, pb_ref, w_ref, near, halo, got,
+    start_own, codes, start_ref, yi_s, dy_ref, pay2, got2, dcc_ref, dbi, rsum_ref,
+    dgain_ref, dskip_ref, end_own, end, tail, rim, rim_in, part, ext, segs, dact, csum,
+    ksum, zbuf, hbuf, own, dhead, rbuf, total, fbuf, alpha_s, cs_s, ady_s, qhi_s, qlo_s,
+    gate_sem, cot_sem, near_send, w_sem, near_sem, halo_sem, send_sem, recv_sem, start_send,
+    grad_send, grad_recv, back_send, rim_send, rim_sem, z_send, z_sem, h_send, h_sem,
+    r_send, r_sem, f_send, f_sem, start_recv, back_recv,
 ):
     me = place()
     c, h, d = lax.axis_index("ctx"), lax.axis_index("head"), lax.axis_index("dp")
@@ -534,23 +429,115 @@
         return carry
 
     lax.fori_loop(0, 16, greet_twin, 0)
+    gate_in = pltpu.make_async_copy(gate_hbm, gate_v, gate_sem)
+    cot_in = pltpu.make_async_copy(cot_hbm, cot_v, cot_sem)
+    gate_in.start()
+    cot_in.start()
+
+    def pack(t, carry):
+        last = xbc_ref[112:128, pl.ds(off(t, 128), 128)].astype(f32)
+        for k in range(3):
+            near[pl.ds((t // 10) * 32 + 10 * k + lax.rem(t, 10), 1), :] = last[13 + k : 14 + k]
+        return carry
+
+    lax.fori_loop(0, 80, pack, 0)
+    for i in range(8):
+        near[32 * i + 30 : 32 * i + 32, :] = jnp.zeros((2, 128), f32)
+    ids = jnp.broadcast_to(seg_ref[...].astype(f32) + 1.0, (T, T)).T
+    near[256:264, :] = jnp.zeros((8, 128), f32)
+    near[256:259, :] = ids[T - 3 :]
+    pl.semaphore_wait(barrier, 63 + 16)
+
+    pltpu.make_async_copy(own_ref, w_ref.at[h], w_sem).start()
+    for k in range(1, 4):
+        pltpu.make_async_remote_copy(
+            src_ref=own_ref, dst_ref=w_ref.at[h], send_sem=near_send, recv_sem=w_sem,
+            device_id=at(me - h + lax.rem(h + k, 4)), device_id_type=MESH,
+        ).start()
+
+    @pl.when(me < 63)
+    def _():
+        pltpu.make_async_remote_copy(
+            src_ref=near, dst_ref=halo, send_sem=near_sem, recv_sem=halo_sem,
+            device_id=at(lax.rem(me + 1, 64)), device_id_type=MESH,
+        ).start()
+
+    @pl.when(me == 0)
+    def _():
+        halo[...] = jnp.zeros_like(halo)
+
+    await_bytes(w_ref, w_sem)
+    await_bytes(w_ref.at[pl.ds(0, 3)], near_send)
+
+    @pl.when(me > 0)
+    def _():
+        await_bytes(halo, halo_sem)
+
+    @pl.when(me < 63)
+    def _():
+        await_bytes(near, near_sem)
+
+    make_prep(halo, w_ref, dt_ref, seg_ref, prep_ref, pb_ref, segs)
+
+    def conv_turn(i, carry):
+        g = turn(me, i)
+        conv_group(g, xbc_ref, halo, w_ref, prep_ref, pb_ref, act_ref, pay_ref, ext)
+        for s in range(8):
+            p = 8 * g + s
+            send_slot(me, p, pay_ref.at[p], got.at[me], send_sem, recv_sem)
+        return carry
+
+    lax.fori_loop(0, 8, conv_turn, 0)
+
+    def forward(i, carry):
+        inner_forward(i, act_ref, prep_ref, yi_s)
+        return carry
+
+    lax.fori_loop(0, 8, forward, 0)
+    await_bytes(got, recv_sem)
+    scan_up(got, start_own)
+
+
+    rsum_ref[...] = jnp.zeros_like(rsum_ref)
+    dskip_ref[...] = jnp.zeros_like(dskip_ref)
+    send_back(me, start_own, codes, start_send, start_recv)
+    gate_in.wait()
+    cot_in.wait()
+
+    def gate_turn(i, carry):
+        g = turn(me, i)
+        await_bytes(codes.at[pl.ds(8 * g, 8)], start_recv.at[g])
+        gate_group(
+            g, act_ref, yi_s, codes, start_ref, gate_v, cot_v, w_ref, pb_ref,
+            dy_ref, dgate_v, pay2, dcc_ref, rsum_ref, dgain_ref, dskip_ref,
+            alpha_s, cs_s, ady_s, qhi_s, qlo_s,
+        )
+        for s in range(8):
+            p = 8 * g + s
+            send_slot(me, p, pay2.at[p], got2.at[me], grad_send, grad_recv)
+        return carry
+
+    lax.fori_loop(0, 8, gate_turn, 0)
+    dgate_out = pltpu.make_async_copy(dgate_v, dgate_hbm, gate_sem)
+    dgate_out.start()
     csum[...] = jnp.zeros_like(csum)
     ksum[...] = jnp.zeros_like(ksum)
     rim[...] = jnp.zeros_like(rim)
 
-    def inner(i, carry):
-        inner_backward(i, act_ref, dy_ref, prep_ref, dcc_ref, dxi, dbi, dci)
-        return carry
-
-    lax.fori_loop(0, 8, inner, 0)
-    pl.semaphore_wait(barrier, 63 + 16)
+    def backward(i, carry):
+        inner_backward(i, act_ref, dy_ref, prep_ref, dcc_ref, yi_s, dbi, dcc_ref)
+        return carry
+
+    lax.fori_loop(0, 8, backward, 0)
+    await_bytes(got2, grad_recv)
+    scan_down(got, got2, end_own)
     send_back(me, end_own, end, back_send, back_recv)
 
-    def one(i, carry):
+    def back_turn(i, carry):
         g = turn(me, i)
         await_bytes(end.at[pl.ds(8 * g, 8)], back_recv.at[g])
         back_group(
-            g, xbc_ref, halo, w_ref, act_ref, dy_ref, dxi, dbi, dci, start_ref, pay_ref, end,
+            g, xbc_ref, halo, w_ref, act_ref, dy_ref, yi_s, dbi, dcc_ref, start_ref, pay_ref, end,
             prep_ref, pb_ref, dgain_ref, dxbc_ref, tail, rim, part, ext, dact, csum, ksum,
         )
         send_slot(
@@ -567,7 +554,7 @@
 
         return carry
 
-    lax.fori_loop(0, 8, one, 0)
+    lax.fori_loop(0, 8, back_turn, 0)
 
     high = (iota((T, T), 0) <= iota((T, T), 1)).astype(f32)
     step, decay = prep_ref[9], prep_ref[10]
@@ -666,25 +653,20 @@
     def _():
         await_bytes(rbuf.at[pl.ds(0, 21)], r_send)
 
+    await_bytes(got.at[pl.ds(0, 63)], send_sem)
+    await_bytes(codes.at[pl.ds(0, 63)], start_send)
+    await_bytes(got2.at[pl.ds(0, 63)], grad_send)
+    dgate_out.wait()
+
+
+def hand_over(*refs):
+    half = len(refs) // 2
+    for src, dst in zip(refs[:half], refs[half:]):
+        dst[...] = src[...]
+
 
 def S(shape, dtype):
     return jax.ShapeDtypeStruct(shape, dtype)
-
-
-def call(kernel, name, ins, outs, scratch, cid):
-    spec = pl.BlockSpec(memory_space=VMEM)
-    return pl.pallas_call(
-        kernel,
-        in_specs=[spec] * len(ins),
-        out_specs=[spec] * len(outs),
-        out_shape=outs,
-        scratch_shapes=scratch,
-        compiler_params=pltpu.CompilerParams(
-            vmem_limit_bytes=56 << 20, collective_id=cid, has_side_effects=True
-        ),
-        cost_estimate=pl.CostEstimate(flops=4 << 30, bytes_accessed=16 << 20, transcendentals=0),
-        name=name,
-    )(*ins)
 
 
 def body(
@@ -701,78 +683,53 @@
         axis=0,
     )
     dma = pltpu.SemaphoreType.DMA
-    act, pay, prep, pb, w_all, halo, starts, tails = call(
-        first_kernel,
-        "conv_states",
-        (xbc, own_w, dt, segment_ids),
-        (
-            S((T, CH), bf16),
-            S((64, 144, 128), bf16),
-            S((12, T, T), f32),
-            S((3, T, 2 * T), bf16),
-            S((4, 6, 2560), f32),
-            S((264, 128), f32),
-            S((64, 144, 128), bf16),
-            S((64, 16, 128), bf16),
-        ),
-        (
+    near = pl.BlockSpec(memory_space=VMEM)
+    far = pl.BlockSpec(memory_space=pl.ANY)
+    outs = (
+        S((T, CH), bf16),
+        S((T, HP), bf16),
+        S((T, HEADS), bf16),
+        S((5, 2560), f32),
+        S((1, 2048), f32),
+        S((3, 32), f32),
+    )
+    results = pl.pallas_call(
+        mixer,
+        in_specs=[near, near, near, near, far, far],
+        out_specs=[near, far, near, near, near, near],
+        out_shape=outs,
+        scratch_shapes=(
+            VMEM((T, HP), bf16),
+            VMEM((T, HP), bf16),
+            VMEM((T, HP), bf16),
+            VMEM((T, CH), bf16),
             VMEM((64, 144, 128), bf16),
+            VMEM((12, T, T), f32),
+            VMEM((3, T, 2 * T), bf16),
+            VMEM((4, 6, 2560), f32),
             VMEM((264, 128), f32),
-            VMEM((136, GW), f32),
-            VMEM((136, 128), f32),
-            dma, dma, dma, dma, dma,
-        ),
-        1,
-    )
-    start, dy, dgate, dcc, rsum, dgain, dskip, ends = call(
-        second_kernel,
-        "gate_norm",
-        (act, starts, tails, gate, cot, w_all, prep, pb),
-        (
-            S((64, 128, 128), bf16),
-            S((T, HP), bf16),
-            S((T, HP), bf16),
-            S((8, T, 128), f32),
-            S((T, HEADS), f32),
-            S((8, 1, XW), f32),
-            S((16, HEADS), f32),
-            S((64, 128, 128), bf16),
-        ),
-        (
+            VMEM((264, 128), f32),
             VMEM((64, 144, 128), bf16),
+            VMEM((64, 144, 128), bf16),
+            VMEM((64, 144, 128), bf16),
+            VMEM((64, 128, 128), bf16),
             VMEM((T, HP), f32),
+            VMEM((T, HP), bf16),
             VMEM((64, 128, 128), bf16),
             VMEM((64, 128, 128), bf16),
-            VMEM((T, XW), f32),
-            VMEM((T, XW), f32),
-            VMEM((T, XW), bf16),
-            VMEM((T, XW), bf16),
-            VMEM((T, XW), bf16),
-            dma, dma((8,)), dma, dma,
-        ),
-        2,
-    )
-    dxbc, ddt, gconv, ggain, gheads = call(
-        third_kernel,
-        "conv_backward",
-        (xbc, halo, w_all, act, dy, dcc, start, pay, ends, prep, pb, rsum, dgain, dskip),
-        (
-            S((T, CH), bf16),
-            S((T, HEADS), bf16),
-            S((5, 2560), f32),
-            S((1, 2048), f32),
-            S((3, 32), f32),
-        ),
-        (
-            VMEM((T, HP), f32),
             VMEM((8, T, 128), f32),
             VMEM((8, T, 128), f32),
+            VMEM((T, HEADS), f32),
+            VMEM((8, 1, XW), f32),
+            VMEM((16, HEADS), f32),
+            VMEM((64, 128, 128), bf16),
             VMEM((64, 128, 128), bf16),
             VMEM((16, CH), f32),
             VMEM((256, 128), f32),
             VMEM((256, 128), f32),
             VMEM((8, 10, 8, 128), f32),
             VMEM((136, GW), f32),
+            VMEM((136, 128), f32),
             VMEM((T, GW), bf16),
             VMEM((T, HEADS), f32),
             VMEM((8, HEADS), f32),
@@ -783,10 +740,37 @@
             VMEM((32, 8, 128), f32),
             VMEM((8, 128), f32),
             VMEM((21, 8, 128), f32),
-            dma, dma((8,)), dma, dma, dma, dma, dma, dma, dma, dma, dma, dma,
+            VMEM((T, XW), f32),
+            VMEM((T, XW), f32),
+            VMEM((T, XW), bf16),
+            VMEM((T, XW), bf16),
+            VMEM((T, XW), bf16),
+            *([dma] * 22),
+            dma((8,)),
+            dma((8,)),
         ),
-        3,
-    )
+        compiler_params=pltpu.CompilerParams(
+            vmem_limit_bytes=58 << 20, collective_id=1, has_side_effects=True
+        ),
+        cost_estimate=pl.CostEstimate(flops=4 << 30, bytes_accessed=16 << 20, transcendentals=0),
+        name="mixer",
+    )(xbc, own_w, dt, segment_ids, gate, cot)
+
+    def cut(shape, dtype):
+        lead = (0,) * (len(shape) - 1)
+        if shape[-1] > 4096:
+            return pl.BlockSpec((shape[0], shape[1] // 8), lambda g: (0, g))
+        return pl.BlockSpec(shape, lambda g: lead + (0,))
+
+    specs = [cut(o.shape, o.dtype) for o in outs]
+    dxbc, dgate, ddt, gconv, ggain, gheads = pl.pallas_call(
+        hand_over,
+        grid=(8,),
+        in_specs=specs,
+        out_specs=specs,
+        out_shape=outs,
+        name="hand_over",
+    )(*results)
     return (dxbc[None], dgate[None], ddt[None], gconv, ggain[0], gheads)
 
 

time: 218 us -> 194 us (0.89)
  Pallas kernels: 207 us -> 190 us
  local copies, waits for them, and re-layouts: 8.94 us -> 1.56 us
    pallas_call x3 -> x2, Pallas kernels: 207 us -> 190 us  [the longest x1 183 us: body(): pl.pallas_call(mixer, in_specs=[near, near, near, near, far, far], out_sp...]
    unnamed x16 -> x0, local copies, waits for them, and re-layouts: 7.38 us -> none
where the time goes in v3:
time: 194 us; the launch traced here: 193 us
  Pallas kernels  190 us (98%)
    pallas_call x1, Pallas kernels, body(): pl.pallas_call(mixer, in_specs=[near, near, near, near, far, far], out_sp...  183 us
    pallas_call x1, Pallas kernels, body(): pl.pallas_call(hand_over, grid=(8,), in_specs=specs, out_specs=specs, out...  6.91 us

profile of v3, /device:TPU:1, one launch (start us, length us, event | category | flops | bytes accessed | tf_op | source)
XLA Modules:
  0.0 193.3 jit_solution(16801352807513501973)
XLA Ops:
  0.6 0.8 reshape.15
  1.4 0.8 concatenate.6
  2.2 1.5 pad_maximum_fusion.own_ref
  3.7 182.7 %mixer.1 = (bf16[128,10240]{1,0:T(8,128)(2,1)}, bf16[128,8192]{1,0:T(8,128)(2,1)}, bf16[128,128]{1,0:T(8,128)(2,1)}, f32[5,2560]{1,0:T(8,128)}, f32[1,2048]{1,0:T(1,128)}, /*index=5*/f32[3,32]{1,0:T(4,128)}) custom-call(bf16[128,10240]{1,0:T(8,128)(2,1)} %bitcast.10, f32[6,2560]{1,0:T(8,128)} %pad_maximum_fusion.own_ref, bf16[128,128]{1,0:T(8,128)(2,1)} %bitcast.15, ...), custom_call_target="tpu_custom_call" | custom-call | flops 4294967296 | bytes 16777216 | tf_op jit(solution)/shard_map/mixer/pallas_call | solution.py:696
  186.4 6.9 %hand_over.1 = (bf16[128,10240]{1,0:T(8,128)(2,1)}, bf16[128,8192]{1,0:T(8,128)(2,1)}, bf16[128,128]{1,0:T(8,128)(2,1)}, f32[5,2560]{1,0:T(8,128)}, f32[1,2048]{1,0:T(1,128)}, /*index=5*/f32[3,32]{1,0:T(4,128)}) custom-call(bf16[128,10240]{1,0:T(8,128)(2,1)} %get-tuple-element.18.refs_0_, bf16[128,8192]{1,0:T(8,128)(2,1)} %get-tuple-element.19.refs_1_, ...), custom_call_target="tpu_custom_call" | custom-call | tf_op jit(solution)/shard_map/hand_over/pallas_call | solution.py:766
  (1 shorter events, 0.0 us)

commit v4 on v3

--- a/solution.py
+++ b/solution.py
@@ -120,9 +120,9 @@
     ]
 
 
-def taps_of(w_ref, g, c):
+def taps_of(w_refs, g, c):
     lanes = pl.ds(pl.multiple_of(lax.rem(g, 2) * GW + 128 * c, 128), 128)
-    return [w_ref[g // 2, k : k + 1, lanes] for k in range(5)]
+    return [w_refs[0][g // 2, k : k + 1, lanes] for k in range(5)]
 
 
 def conv(wins, taps):
@@ -132,14 +132,13 @@
     return pre
 
 
-def params(w_ref, row):
-    first = 2048 + 32 * row
-    return jnp.concatenate([w_ref[q, 5:6, first : first + 32] for q in range(4)], axis=1)
-
-
-def make_prep(halo, w_ref, dt_ref, seg_ref, prep_ref, pb_ref, segs):
-    rate = jnp.exp(params(w_ref, 0))
-    dtb = dt_ref[...].astype(f32) + params(w_ref, 1)
+def params(w_refs, row):
+    return jnp.concatenate([w_refs[2][q, row : row + 1, :32] for q in range(4)], axis=1)
+
+
+def make_prep(halo, w_refs, dt_ref, seg_ref, prep_ref, pb_ref, segs):
+    rate = jnp.exp(params(w_refs, 0))
+    dtb = dt_ref[...].astype(f32) + params(w_refs, 1)
     step = jnp.maximum(dtb, 0.0) + jnp.log1p(jnp.exp(-jnp.abs(dtb)))
     decay = -step * rate
     rows, cols = iota((T, T), 0), iota((T, T), 1)
@@ -170,18 +169,21 @@
         hi, lo = split(v)
         pb_ref[i, :, :T] = hi
         pb_ref[i, :, T:] = lo
-    both = jnp.where(rows == 0, params(w_ref, 2), keep)
+    both = jnp.where(rows == 0, params(w_refs, 2), keep)
     hi, lo = split(both)
     pb_ref[2, :, :T] = hi
     pb_ref[2, :, T:] = lo
 
 
-def conv_group(g, xbc_ref, halo, w_ref, prep_ref, pb_ref, act_ref, pay_ref, ext):
+def conv_group(g, xbc_ref, halo, w_refs, prep_ref, pb_ref, act_ref, slope, pay_ref, keep_own, ext):
     load_ext(g, ext, xbc_ref, halo)
     base = off(g, GW)
     for c in range(GW // 128):
-        pre = conv(windows(ext, prep_ref, slice(128 * c, 128 * c + 128)), taps_of(w_ref, g, c))
-        act_ref[:, pl.ds(base + 128 * c, 128)] = (pre * sigmoid(pre)).astype(bf16)
+        pre = conv(windows(ext, prep_ref, slice(128 * c, 128 * c + 128)), taps_of(w_refs, g, c))
+        sg = sigmoid(pre)
+        value = pre * sg
+        act_ref[:, pl.ds(base + 128 * c, 128)] = value.astype(bf16)
+        slope[:, pl.ds(base + 128 * c, 128)] = sg + value * (1.0 - sg)
     sel = selector(g)
     omega = mm(pb_ref[1], twice(sel))
     x_ref, b_ref, _ = parts_of(act_ref, g)
@@ -189,11 +191,11 @@
     state = mm(b_ref[...], weighted, TN).astype(bf16)
     khi = mm(pb_ref[2, :16, :T], sel)
     klo = mm(pb_ref[2, :16, T:], sel)
-    tail = jnp.where(iota((16, XW), 0) == 0, khi[1:2], klo[1:2]).astype(bf16)
+    keep = khi[1:2] + klo[1:2]
     for i in range(8):
         lanes = slice(128 * i, 128 * i + 128)
-        pay_ref[8 * g + i, :128, :] = state[:, lanes]
-        pay_ref[8 * g + i, 128:, :] = tail[:, lanes]
+        pay_ref[8 * g + i] = state[:, lanes]
+        keep_own[8 * g + i] = keep[:, lanes]
 
 
 def parts_of(act_ref, g):
@@ -211,32 +213,27 @@
     return jnp.concatenate([jnp.where(left, v, zero), jnp.where(left, zero, v)], axis=0)
 
 
-def scan_up(got_ref, start_ref):
+def scan_up(keep_in, got_ref, start_ref, scale_ref):
     def one(j, state):
         top = jnp.maximum(jnp.max(jnp.abs(state), axis=0, keepdims=True) * 1.01, TINY)
-        scale = top.astype(bf16).astype(f32)
-        start_ref[j, :128, :] = jnp.exp2(state * (SPAN / scale)).astype(bf16)
-        start_ref[j, 128:, :] = jnp.broadcast_to(scale, (16, 128)).astype(bf16)
-        tail = got_ref[j, 128:, :].astype(f32)
-        keep = tail[0:1] + tail[1:2]
-        return keep * state + got_ref[j, :128, :].astype(f32)
+        start_ref[j] = jnp.exp2(state * (SPAN / top)).astype(bf16)
+        scale_ref[j] = top
+        return keep_in[j] * state + got_ref[j].astype(f32)
 
     lax.fori_loop(0, 64, one, jnp.zeros((128, 128), f32))
 
 
-def scan_down(got_up, got_ref, end_ref):
+def scan_down(keep_in, got_ref, end_ref):
     def one(i, grad):
         j = 63 - i
         end_ref[j] = grad.astype(bf16)
-        tail = got_up[j, 128:, :].astype(f32)
-        keep = tail[0:1] + tail[1:2]
-        return keep * grad + got_ref[j].astype(f32)
+        return keep_in[j] * grad + got_ref[j].astype(f32)
 
     lax.fori_loop(0, 64, one, jnp.zeros((128, 128), f32))
 
 
 def wide(slots_ref, g):
-    return jnp.concatenate([slots_ref[8 * g + i, :128, :] for i in range(8)], axis=1)
+    return jnp.concatenate([slots_ref[8 * g + i] for i in range(8)], axis=1)
 
 
 def inner_forward(g, act_ref, prep_ref, y_ref):
@@ -256,16 +253,16 @@
         )
 
 
-def decode(code_ref, g):
+def decode(code_ref, scale_ref, g):
     codes = wide(code_ref, g).astype(f32)
-    scale = jnp.concatenate([code_ref[8 * g + i, 128:, :] for i in range(8)], axis=1)
-    return jnp.log2(codes) * (scale[0:1].astype(f32) * (1.0 / SPAN))
+    scale = jnp.concatenate([scale_ref[8 * g + i] for i in range(8)], axis=1)
+    return jnp.log2(codes) * (scale * (1.0 / SPAN))
 
 
 def gate_group(
-    g, act_ref, yi_ref, code_ref, start_ref, gate_ref, cot_ref, w_ref, pb_ref,
+    g, act_ref, yi_ref, code_ref, scale_ref, start_ref, gate_ref, cot_ref, w_refs, pb_ref,
     dy_ref, dgate_ref, pay_ref, dcc_ref, rsum_ref, dgain_ref, dskip_ref,
-    alpha_s, cs_s, ady_s, qhi_s, qlo_s,
+    alpha_s, cs_s, ady_s, ady_lo, qhi_s, qlo_s,
 ):
     x_ref, _, c_ref = parts_of(act_ref, g)
     base = pl.ds(off(g, XW), XW)
@@ -273,13 +270,13 @@
     dy_ref, dgate_ref = dy_ref.at[:, base], dgate_ref.at[:, base]
     sel = selector(g)
     both = twice(sel)
-    start, start_lo = split(decode(code_ref, g))
+    start, start_lo = split(decode(code_ref, scale_ref, g))
     for i in range(8):
         start_ref[8 * g + i] = start[:, 128 * i : 128 * i + 128]
     cs_s[...] = mm(c_ref[...], start) + mm(c_ref[...], start_lo)
     alpha_s[...] = mm(pb_ref[0], both)
     skip = mm(pb_ref[2, :16, :], both)[0:1]
-    gain = w_ref[g // 2, 5:6, pl.ds(off(lax.rem(g, 2), XW), XW)]
+    gain = w_refs[1][g // 2, :, pl.ds(off(lax.rem(g, 2), XW), XW)]
     dgain = jnp.zeros((16, XW), f32)
     dskip = jnp.zeros((16, XW), f32)
     for r in range(8):
@@ -303,29 +300,35 @@
         dy_ref[rows, :] = dy
         dgate_ref[rows, :] = (dgated * ssm * (sg + sl * (1.0 - sg))).astype(bf16)
         dyf = dy.astype(f32)
-        ady_s[rows, :] = (alpha * dyf).astype(bf16)
+        hi, lo = split(alpha * dyf)
+        ady_s[rows, :] = hi
+        ady_lo[rows, :] = lo
         hi, lo = split(dyf * yssm)
         qhi_s[rows, :] = hi
         qlo_s[rows, :] = lo
         dskip = dskip + dyf * x
     ady = ady_s[...]
-    dstart = mm(c_ref[...], ady, TN).astype(bf16)
+    dstart = (mm(c_ref[...], ady, TN) + mm(c_ref[...], ady_lo[...], TN)).astype(bf16)
     for i in range(8):
         pay_ref[8 * g + i] = dstart[:, 128 * i : 128 * i + 128]
-    dcc_ref[g] = mm(ady, start, NT) + mm(ady, start_lo, NT)
+    dcc_ref[g] = mm(ady, start, NT) + mm(ady, start_lo, NT) + mm(ady_lo[...], start, NT)
     rsum_ref[...] += mm(qhi_s[...], sel, NT) + mm(qlo_s[...], sel, NT)
     dskip_ref[...] += head_sums(dskip, sel)
     dgain_ref[g] = jnp.sum(dgain, axis=0, keepdims=True)
 
 
-def send_back(me, values, landing, send_sem, recv_sems):
+def send_turn(me, i, pairs):
     mine = me // 8
-
+    group = lax.rem(mine + 8 - i, 8)
+    for s in range(8):
+        p = 8 * group + s
+        for values, landing, send_sem, recv_sems in pairs:
+            send_slot(me, p, values.at[p], landing.at[me], send_sem, recv_sems.at[mine])
+
+
+def send_all(me, pairs):
     def one(i, carry):
-        group = lax.rem(mine + 8 - i, 8)
-        for s in range(8):
-            p = 8 * group + s
-            send_slot(me, p, values.at[p], landing.at[me], send_sem, recv_sems.at[mine])
+        send_turn(me, i, pairs)
         return carry
 
     lax.fori_loop(0, 8, one, 0)
@@ -355,8 +358,8 @@
 
 
 def back_group(
-    g, xbc_ref, halo, w_ref, act_ref, dy_ref, dxi, dbi, dci, start_ref, pay_ref, end,
-    prep_ref, pb_ref, dgain_ref, dxbc_ref, tail, rim, part, ext, dact, csum, ksum,
+    g, xbc_ref, halo, w_refs, act_ref, dy_ref, dxi, dbi, dci, start_ref, pay_ref, end,
+    slope, prep_ref, pb_ref, dgain_ref, dxbc_ref, tail, rim, part, ext, dact, csum, ksum,
 ):
     x_ref, b_ref, _ = parts_of(act_ref, g)
     base = pl.ds(off(g, XW), XW)
@@ -380,13 +383,9 @@
     for c in range(GW // 128):
         lanes = slice(128 * c, 128 * c + 128)
         wide_lanes = pl.ds(off(g, GW) + 128 * c, 128)
-        wins = windows(ext, prep_ref, lanes)
-        taps = taps_of(w_ref, g, c)
-        pre = conv(wins, taps)
-        sg = sigmoid(pre)
-        dpre = dact[:, lanes].astype(f32) * (sg + pre * sg * (1.0 - sg))
-        for k in range(4):
-            part[g, c, k : k + 1, :] = jnp.sum(dpre * wins[k], axis=0, keepdims=True)
+        taps = taps_of(w_refs, g, c)
+        dpre = dact[:, lanes].astype(f32) * slope[:, wide_lanes]
+        part[g, c, 3:4, :] = jnp.sum(dpre * ext[8:136, lanes], axis=0, keepdims=True)
         part[g, c, 4:5, :] = jnp.sum(dpre, axis=0, keepdims=True)
         if c < 8:
             part[g, c, 5:6, :] = dgain_ref[g, :, lanes]
@@ -397,7 +396,11 @@
         over = jnp.zeros((8, 128), f32)
         for k in range(3):
             far = 3 - k
-            moved = pltpu.roll(taps[k] * dpre * prep_ref[6 + k], T - far, 0)
+            used = dpre * prep_ref[6 + k]
+            part[g, c, k : k + 1, :] = jnp.sum(
+                used * ext[5 + k : 133 + k, lanes], axis=0, keepdims=True
+            )
+            moved = taps[k] * pltpu.roll(used, T - far, 0)
             inside = rows < T - far
             total = total + jnp.where(inside, moved, 0.0)
             over = over + jnp.where(inside, 0.0, moved)[T - 8 :]
@@ -408,15 +411,16 @@
 
 
 def mixer(
-    xbc_ref, own_ref, dt_ref, seg_ref, gate_hbm, cot_hbm,
+    xbc_ref, own_conv, own_gain, own_head, dt_ref, seg_ref, gate_hbm, cot_hbm,
     dxbc_ref, dgate_hbm, ddt_ref, gconv_ref, ggain_ref, gheads_ref,
-    gate_v, cot_v, dgate_v, act_ref, pay_ref, prep_ref, pb_ref, w_ref, near, halo, got,
+    gate_v, cot_v, dgate_v, act_ref, pay_ref, prep_ref, pb_ref, w_conv, w_gain, w_head, near, halo, got,
     start_own, codes, start_ref, yi_s, dy_ref, pay2, got2, dcc_ref, dbi, rsum_ref,
     dgain_ref, dskip_ref, end_own, end, tail, rim, rim_in, part, ext, segs, dact, csum,
     ksum, zbuf, hbuf, own, dhead, rbuf, total, fbuf, alpha_s, cs_s, ady_s, qhi_s, qlo_s,
-    gate_sem, cot_sem, near_send, w_sem, near_sem, halo_sem, send_sem, recv_sem, start_send,
+    slope, ady_lo, keep_own, keep_in, scale_own, scales,
+    keep_send, keep_recv, scale_send, gate_sem, cot_sem, near_sem, halo_sem, send_sem, recv_sem, start_send,
     grad_send, grad_recv, back_send, rim_send, rim_sem, z_send, z_sem, h_send, h_sem,
-    r_send, r_sem, f_send, f_sem, start_recv, back_recv,
+    r_send, r_sem, f_send, f_sem, near_send, w_sem, start_recv, back_recv, scale_recv,
 ):
     me = place()
     c, h, d = lax.axis_index("ctx"), lax.axis_index("head"), lax.axis_index("dp")
@@ -434,13 +438,11 @@
     gate_in.start()
     cot_in.start()
 
-    def pack(t, carry):
-        last = xbc_ref[112:128, pl.ds(off(t, 128), 128)].astype(f32)
+    for t in range(80):
+        last = xbc_ref[112:128, 128 * t : 128 * t + 128].astype(f32)
+        row = (t // 10) * 32 + t % 10
         for k in range(3):
-            near[pl.ds((t // 10) * 32 + 10 * k + lax.rem(t, 10), 1), :] = last[13 + k : 14 + k]
-        return carry
-
-    lax.fori_loop(0, 80, pack, 0)
+            near[row + 10 * k : row + 10 * k + 1, :] = last[13 + k : 14 + k]
     for i in range(8):
         near[32 * i + 30 : 32 * i + 32, :] = jnp.zeros((2, 128), f32)
     ids = jnp.broadcast_to(seg_ref[...].astype(f32) + 1.0, (T, T)).T
@@ -448,12 +450,15 @@
     near[256:259, :] = ids[T - 3 :]
     pl.semaphore_wait(barrier, 63 + 16)
 
-    pltpu.make_async_copy(own_ref, w_ref.at[h], w_sem).start()
-    for k in range(1, 4):
-        pltpu.make_async_remote_copy(
-            src_ref=own_ref, dst_ref=w_ref.at[h], send_sem=near_send, recv_sem=w_sem,
-            device_id=at(me - h + lax.rem(h + k, 4)), device_id_type=MESH,
-        ).start()
+    w_refs = (w_conv, w_gain, w_head)
+    for n, own_w in enumerate((own_conv, own_gain, own_head)):
+        pltpu.make_async_copy(own_w, w_refs[n].at[h], w_sem.at[n]).start()
+        for k in range(1, 4):
+            pltpu.make_async_remote_copy(
+                src_ref=own_w, dst_ref=w_refs[n].at[h], send_sem=near_send.at[n],
+                recv_sem=w_sem.at[n], device_id=at(me - h + lax.rem(h + k, 4)),
+                device_id_type=MESH,
+            ).start()
 
     @pl.when(me < 63)
     def _():
@@ -466,8 +471,9 @@
     def _():
         halo[...] = jnp.zeros_like(halo)
 
-    await_bytes(w_ref, w_sem)
-    await_bytes(w_ref.at[pl.ds(0, 3)], near_send)
+    for n in range(3):
+        await_bytes(w_refs[n], w_sem.at[n])
+        await_bytes(w_refs[n].at[pl.ds(0, 3)], near_send.at[n])
 
     @pl.when(me > 0)
     def _():
@@ -477,13 +483,14 @@
     def _():
         await_bytes(near, near_sem)
 
-    make_prep(halo, w_ref, dt_ref, seg_ref, prep_ref, pb_ref, segs)
+    make_prep(halo, w_refs, dt_ref, seg_ref, prep_ref, pb_ref, segs)
 
     def conv_turn(i, carry):
         g = turn(me, i)
-        conv_group(g, xbc_ref, halo, w_ref, prep_ref, pb_ref, act_ref, pay_ref, ext)
+        conv_group(g, xbc_ref, halo, w_refs, prep_ref, pb_ref, act_ref, slope, pay_ref, keep_own, ext)
         for s in range(8):
             p = 8 * g + s
+            send_slot(me, p, keep_own.at[p], keep_in.at[me], keep_send, keep_recv)
             send_slot(me, p, pay_ref.at[p], got.at[me], send_sem, recv_sem)
         return carry
 
@@ -494,23 +501,29 @@
         return carry
 
     lax.fori_loop(0, 8, forward, 0)
+    await_bytes(keep_in, keep_recv)
     await_bytes(got, recv_sem)
-    scan_up(got, start_own)
+    scan_up(keep_in, got, start_own, scale_own)
 
 
     rsum_ref[...] = jnp.zeros_like(rsum_ref)
     dskip_ref[...] = jnp.zeros_like(dskip_ref)
-    send_back(me, start_own, codes, start_send, start_recv)
+    starts = (
+        (scale_own, scales, scale_send, scale_recv),
+        (start_own, codes, start_send, start_recv),
+    )
+    send_all(me, starts)
     gate_in.wait()
     cot_in.wait()
 
     def gate_turn(i, carry):
         g = turn(me, i)
+        await_bytes(scales.at[pl.ds(8 * g, 8)], scale_recv.at[g])
         await_bytes(codes.at[pl.ds(8 * g, 8)], start_recv.at[g])
         gate_group(
-            g, act_ref, yi_s, codes, start_ref, gate_v, cot_v, w_ref, pb_ref,
+            g, act_ref, yi_s, codes, scales, start_ref, gate_v, cot_v, w_refs, pb_ref,
             dy_ref, dgate_v, pay2, dcc_ref, rsum_ref, dgain_ref, dskip_ref,
-            alpha_s, cs_s, ady_s, qhi_s, qlo_s,
+            alpha_s, cs_s, ady_s, ady_lo, qhi_s, qlo_s,
         )
         for s in range(8):
             p = 8 * g + s
@@ -530,15 +543,16 @@
 
     lax.fori_loop(0, 8, backward, 0)
     await_bytes(got2, grad_recv)
-    scan_down(got, got2, end_own)
-    send_back(me, end_own, end, back_send, back_recv)
+    scan_down(keep_in, got2, end_own)
+    ends = ((end_own, end, back_send, back_recv),)
+    send_all(me, ends)
 
     def back_turn(i, carry):
         g = turn(me, i)
         await_bytes(end.at[pl.ds(8 * g, 8)], back_recv.at[g])
         back_group(
-            g, xbc_ref, halo, w_ref, act_ref, dy_ref, yi_s, dbi, dcc_ref, start_ref, pay_ref, end,
-            prep_ref, pb_ref, dgain_ref, dxbc_ref, tail, rim, part, ext, dact, csum, ksum,
+            g, xbc_ref, halo, w_refs, act_ref, dy_ref, yi_s, dbi, dcc_ref, start_ref, pay_ref, end,
+            slope, prep_ref, pb_ref, dgain_ref, dxbc_ref, tail, rim, part, ext, dact, csum, ksum,
         )
         send_slot(
             me, me - h + g // 2, part.at[g], zbuf.at[h, lax.rem(g, 2)], z_send, z_sem
@@ -561,7 +575,7 @@
     col = csum[...]
     dlog = mm(high, rsum_ref[...] - col, NN, lax.Precision.HIGHEST)
     dlog = dlog + jnp.sum(ksum[...], axis=0, keepdims=True)
-    dstep = col / step - dlog * jnp.exp(params(w_ref, 0))
+    dstep = col / step - dlog * jnp.exp(params(w_refs, 0))
     ddt = dstep * prep_ref[11]
     ddt_ref[...] = ddt.astype(bf16)
     dhead[0:1, :] = jnp.sum(dlog * decay, axis=0, keepdims=True)
@@ -601,6 +615,16 @@
 
     lax.fori_loop(0, 21, spread, 0)
 
+    @pl.when(me < 63)
+    def _():
+        await_bytes(rim_in, rim_sem)
+        for t in range(80):
+            lanes = slice(128 * t, 128 * t + 128)
+            row = (t // 10) * 32 + t % 10
+            for k in range(3):
+                tail[13 + k : 14 + k, lanes] += rim_in[row + 10 * k : row + 10 * k + 1, :]
+            dxbc_ref[112:128, lanes] = tail[:, lanes].astype(bf16)
+
     @pl.when(rank < 21)
     def _():
         await_bytes(rbuf, r_sem)
@@ -611,20 +635,6 @@
             return carry
 
         lax.fori_loop(0, 32, share, 0)
-
-    @pl.when(me < 63)
-    def _():
-        await_bytes(rim_in, rim_sem)
-
-        def fix(t, carry):
-            lanes = pl.ds(off(t, 128), 128)
-            for k in range(3):
-                row = rim_in[pl.ds((t // 10) * 32 + 10 * k + lax.rem(t, 10), 1), :]
-                tail[13 + k : 14 + k, lanes] += row
-            dxbc_ref[112:128, lanes] = tail[:, lanes].astype(bf16)
-            return carry
-
-        lax.fori_loop(0, 80, fix, 0)
 
     await_bytes(fbuf, f_sem)
     for q in range(2):
@@ -653,6 +663,8 @@
     def _():
         await_bytes(rbuf.at[pl.ds(0, 21)], r_send)
 
+    await_bytes(keep_in.at[pl.ds(0, 63)], keep_send)
+    await_bytes(scales.at[pl.ds(0, 63)], scale_send)
     await_bytes(got.at[pl.ds(0, 63)], send_sem)
     await_bytes(codes.at[pl.ds(0, 63)], start_send)
     await_bytes(got2.at[pl.ds(0, 63)], grad_send)
@@ -673,15 +685,7 @@
     xbc_raw, gate_raw, dt_raw, segment_ids, conv_weight, norm_gain, head_params, out_cotangent
 ):
     xbc, gate, dt, cot = xbc_raw[0], gate_raw[0], dt_raw[0], out_cotangent[0]
-    own_w = jnp.concatenate(
-        [
-            conv_weight,
-            jnp.concatenate(
-                [norm_gain[None], head_params.reshape(1, 96), jnp.zeros((1, 416), f32)], axis=1
-            ),
-        ],
-        axis=0,
-    )
+    own_head = jnp.pad(head_params, ((0, 5), (0, 96)))
     dma = pltpu.SemaphoreType.DMA
     near = pl.BlockSpec(memory_space=VMEM)
     far = pl.BlockSpec(memory_space=pl.ANY)
@@ -695,7 +699,7 @@
     )
     results = pl.pallas_call(
         mixer,
-        in_specs=[near, near, near, near, far, far],
+        in_specs=[near, near, near, near, near, near, far, far],
         out_specs=[near, far, near, near, near, near],
         out_shape=outs,
         scratch_shapes=(
@@ -703,15 +707,17 @@
             VMEM((T, HP), bf16),
             VMEM((T, HP), bf16),
             VMEM((T, CH), bf16),
-            VMEM((64, 144, 128), bf16),
+            VMEM((64, 128, 128), bf16),
             VMEM((12, T, T), f32),
             VMEM((3, T, 2 * T), bf16),
-            VMEM((4, 6, 2560), f32),
+            VMEM((4, 5, 2560), f32),
+            VMEM((4, 1, 2048), f32),
+            VMEM((4, 8, 128), f32),
             VMEM((264, 128), f32),
             VMEM((264, 128), f32),
-            VMEM((64, 144, 128), bf16),
-            VMEM((64, 144, 128), bf16),
-            VMEM((64, 144, 128), bf16),
+            VMEM((64, 128, 128), bf16),
+            VMEM((64, 128, 128), bf16),
+            VMEM((64, 128, 128), bf16),
             VMEM((64, 128, 128), bf16),
             VMEM((T, HP), f32),
             VMEM((T, HP), bf16),
@@ -745,7 +751,13 @@
             VMEM((T, XW), bf16),
             VMEM((T, XW), bf16),
             VMEM((T, XW), bf16),
-            *([dma] * 22),
+            VMEM((T, CH), f32),
+            VMEM((T, XW), bf16),
+            *([VMEM((64, 1, 128), f32)] * 4),
+            *([dma] * 23),
+            dma((3,)),
+            dma((3,)),
+            dma((8,)),
             dma((8,)),
             dma((8,)),
         ),
@@ -754,18 +766,18 @@
         ),
         cost_estimate=pl.CostEstimate(flops=4 << 30, bytes_accessed=16 << 20, transcendentals=0),
         name="mixer",
-    )(xbc, own_w, dt, segment_ids, gate, cot)
+    )(xbc, conv_weight, norm_gain[None], own_head, dt, segment_ids, gate, cot)
 
     def cut(shape, dtype):
         lead = (0,) * (len(shape) - 1)
         if shape[-1] > 4096:
-            return pl.BlockSpec((shape[0], shape[1] // 8), lambda g: (0, g))
+            return pl.BlockSpec((shape[0], shape[1] // 4), lambda g: (0, g))
         return pl.BlockSpec(shape, lambda g: lead + (0,))
 
     specs = [cut(o.shape, o.dtype) for o in outs]
     dxbc, dgate, ddt, gconv, ggain, gheads = pl.pallas_call(
         hand_over,
-        grid=(8,),
+        grid=(4,),
         in_specs=specs,
         out_specs=specs,
         out_shape=outs,

time: 194 us -> 183 us (0.943)
  Pallas kernels: 190 us -> 180 us
    pallas_call x2, Pallas kernels: 190 us -> 180 us  [the longest x1 175 us: body(): pl.pallas_call(mixer, in_specs=[near, near, near, near, near, near, far,...]
where the time goes in v4:
time: 183 us; the launch traced here: 182 us
  Pallas kernels  180 us (98%)
    pallas_call x1, Pallas kernels, body(): pl.pallas_call(mixer, in_specs=[near, near, near, near, near, near, far,...  175 us
    pallas_call x1, Pallas kernels, body(): pl.pallas_call(hand_over, grid=(4,), in_specs=specs, out_specs=specs, out...  5.06 us

profile of v4, /device:TPU:1, one launch (start us, length us, event | category | flops | bytes accessed | tf_op | source)
XLA Modules:
  0.0 182.4 jit_solution(4283634638051730365)
XLA Ops:
  0.6 1.3 pad.4.own_head
  1.9 175.4 %mixer.1 = (bf16[128,10240]{1,0:T(8,128)(2,1)}, bf16[128,8192]{1,0:T(8,128)(2,1)}, bf16[128,128]{1,0:T(8,128)(2,1)}, f32[5,2560]{1,0:T(8,128)}, f32[1,2048]{1,0:T(1,128)}, /*index=5*/f32[3,32]{1,0:T(4,128)}) custom-call(bf16[128,10240]{1,0:T(8,128)(2,1)} %bitcast.9, f32[5,2560]{1,0:T(8,128)} %own_conv.1, f32[1,2048]{1,0:T(1,128)} %bitcast.16, ...), custom_call_target="tpu_custom_call" | custom-call | flops 4294967296 | bytes 16777216 | tf_op jit(solution)/shard_map/mixer/pallas_call | solution.py:700
  177.4 5.1 %hand_over.1 = (bf16[128,10240]{1,0:T(8,128)(2,1)}, bf16[128,8192]{1,0:T(8,128)(2,1)}, bf16[128,128]{1,0:T(8,128)(2,1)}, f32[5,2560]{1,0:T(8,128)}, f32[1,2048]{1,0:T(1,128)}, /*index=5*/f32[3,32]{1,0:T(4,128)}) custom-call(bf16[128,10240]{1,0:T(8,128)(2,1)} %get-tuple-element.18.refs_0_, bf16[128,8192]{1,0:T(8,128)(2,1)} %get-tuple-element.19.refs_1_, ...), custom_call_target="tpu_custom_call" | custom-call | tf_op jit(solution)/shard_map/hand_over/pallas_call | solution.py:778

commit v5 on v4

--- a/solution.py
+++ b/solution.py
@@ -450,6 +450,13 @@
     near[256:259, :] = ids[T - 3 :]
     pl.semaphore_wait(barrier, 63 + 16)
 
+    @pl.when(me < 63)
+    def _():
+        pltpu.make_async_remote_copy(
+            src_ref=near, dst_ref=halo, send_sem=near_sem, recv_sem=halo_sem,
+            device_id=at(lax.rem(me + 1, 64)), device_id_type=MESH,
+        ).start()
+
     w_refs = (w_conv, w_gain, w_head)
     for n, own_w in enumerate((own_conv, own_gain, own_head)):
         pltpu.make_async_copy(own_w, w_refs[n].at[h], w_sem.at[n]).start()
@@ -459,13 +466,6 @@
                 recv_sem=w_sem.at[n], device_id=at(me - h + lax.rem(h + k, 4)),
                 device_id_type=MESH,
             ).start()
-
-    @pl.when(me < 63)
-    def _():
-        pltpu.make_async_remote_copy(
-            src_ref=near, dst_ref=halo, send_sem=near_sem, recv_sem=halo_sem,
-            device_id=at(lax.rem(me + 1, 64)), device_id_type=MESH,
-        ).start()
 
     @pl.when(me == 0)
     def _():

time: 183 us -> 180 us (0.984)
  Pallas kernels: 180 us -> 177 us
    pallas_call x1, Pallas kernels: 175 us -> 172 us  [body(): pl.pallas_call(mixer, in_specs=[near, near, near, near, near, near, far,...]
where the time goes in v5:
time: 180 us; the launch traced here: 179 us
  Pallas kernels  177 us (98%)
    pallas_call x1, Pallas kernels, body(): pl.pallas_call(mixer, in_specs=[near, near, near, near, near, near, far,...  172 us
    pallas_call x1, Pallas kernels, body(): pl.pallas_call(hand_over, grid=(4,), in_specs=specs, out_specs=specs, out...  5.06 us

profile of v5, /device:TPU:1, one launch (start us, length us, event | category | flops | bytes accessed | tf_op | source)
XLA Modules:
  0.0 179.3 jit_solution(1943702651108287391)
XLA Ops:
  0.6 1.3 pad.4.own_head
  1.9 172.3 %mixer.1 = (bf16[128,10240]{1,0:T(8,128)(2,1)}, bf16[128,8192]{1,0:T(8,128)(2,1)}, bf16[128,128]{1,0:T(8,128)(2,1)}, f32[5,2560]{1,0:T(8,128)}, f32[1,2048]{1,0:T(1,128)}, /*index=5*/f32[3,32]{1,0:T(4,128)}) custom-call(bf16[128,10240]{1,0:T(8,128)(2,1)} %bitcast.9, f32[5,2560]{1,0:T(8,128)} %own_conv.1, f32[1,2048]{1,0:T(1,128)} %bitcast.16, ...), custom_call_target="tpu_custom_call" | custom-call | flops 4294967296 | bytes 16777216 | tf_op jit(solution)/shard_map/mixer/pallas_call | solution.py:700
  174.2 5.1 %hand_over.1 = (bf16[128,10240]{1,0:T(8,128)(2,1)}, bf16[128,8192]{1,0:T(8,128)(2,1)}, bf16[128,128]{1,0:T(8,128)(2,1)}, f32[5,2560]{1,0:T(8,128)}, f32[1,2048]{1,0:T(1,128)}, /*index=5*/f32[3,32]{1,0:T(4,128)}) custom-call(bf16[128,10240]{1,0:T(8,128)(2,1)} %get-tuple-element.18.refs_0_, bf16[128,8192]{1,0:T(8,128)(2,1)} %get-tuple-element.19.refs_1_, ...), custom_call_target="tpu_custom_call" | custom-call | tf_op jit(solution)/shard_map/hand_over/pallas_call | solution.py:778

commit v6 on v5

--- a/solution.py
+++ b/solution.py
@@ -458,7 +458,7 @@
         ).start()
 
     w_refs = (w_conv, w_gain, w_head)
-    for n, own_w in enumerate((own_conv, own_gain, own_head)):
+    for n, own_w in ((2, own_head), (0, own_conv), (1, own_gain)):
         pltpu.make_async_copy(own_w, w_refs[n].at[h], w_sem.at[n]).start()
         for k in range(1, 4):
             pltpu.make_async_remote_copy(
@@ -471,17 +471,12 @@
     def _():
         halo[...] = jnp.zeros_like(halo)
 
-    for n in range(3):
+    for n in (0, 2):
         await_bytes(w_refs[n], w_sem.at[n])
-        await_bytes(w_refs[n].at[pl.ds(0, 3)], near_send.at[n])
 
     @pl.when(me > 0)
     def _():
         await_bytes(halo, halo_sem)
-
-    @pl.when(me < 63)
-    def _():
-        await_bytes(near, near_sem)
 
     make_prep(halo, w_refs, dt_ref, seg_ref, prep_ref, pb_ref, segs)
 
@@ -515,6 +510,7 @@
     send_all(me, starts)
     gate_in.wait()
     cot_in.wait()
+    await_bytes(w_gain, w_sem.at[1])
 
     def gate_turn(i, carry):
         g = turn(me, i)
@@ -615,6 +611,17 @@
 
     lax.fori_loop(0, 21, spread, 0)
 
+    @pl.when(rank < 21)
+    def _():
+        await_bytes(rbuf, r_sem)
+        total[...] = jnp.sum(rbuf[...], axis=0)
+
+        def share(k, carry):
+            to_rank(lax.rem(rank + k, 32), total, fbuf.at[rank], f_send, f_sem)
+            return carry
+
+        lax.fori_loop(0, 32, share, 0)
+
     @pl.when(me < 63)
     def _():
         await_bytes(rim_in, rim_sem)
@@ -624,17 +631,6 @@
             for k in range(3):
                 tail[13 + k : 14 + k, lanes] += rim_in[row + 10 * k : row + 10 * k + 1, :]
             dxbc_ref[112:128, lanes] = tail[:, lanes].astype(bf16)
-
-    @pl.when(rank < 21)
-    def _():
-        await_bytes(rbuf, r_sem)
-        total[...] = jnp.sum(rbuf[...], axis=0)
-
-        def share(k, carry):
-            to_rank(lax.rem(rank + k, 32), total, fbuf.at[rank], f_send, f_sem)
-            return carry
-
-        lax.fori_loop(0, 32, share, 0)
 
     await_bytes(fbuf, f_sem)
     for q in range(2):
@@ -662,6 +658,13 @@
     @pl.when(rank >= 21)
     def _():
         await_bytes(rbuf.at[pl.ds(0, 21)], r_send)
+
+    for n in range(3):
+        await_bytes(w_refs[n].at[pl.ds(0, 3)], near_send.at[n])
+
+    @pl.when(me < 63)
+    def _():
+        await_bytes(near, near_sem)
 
     await_bytes(keep_in.at[pl.ds(0, 63)], keep_send)
     await_bytes(scales.at[pl.ds(0, 63)], scale_send)

time: 180 us -> 182 us (1.011)
  Pallas kernels: 177 us -> 180 us
    pallas_call x1, Pallas kernels: 172 us -> 175 us  [body(): pl.pallas_call(mixer, in_specs=[near, near, near, near, near, near, far,...]
where the time goes in v6:
time: 182 us
  Pallas kernels  180 us (99%)
    pallas_call x1, Pallas kernels, body(): pl.pallas_call(mixer, in_specs=[near, near, near, near, near, near, far,...  175 us
    pallas_call x1, Pallas kernels, body(): pl.pallas_call(hand_over, grid=(4,), in_specs=specs, out_specs=specs, out...  5.06 us

profile of v6, /device:TPU:1, one launch (start us, length us, event | category | flops | bytes accessed | tf_op | source)
XLA Modules:
  0.0 182.2 jit_solution(14675443218478691432)
XLA Ops:
  0.6 1.3 pad.4.own_head
  1.9 175.3 %mixer.1 = (bf16[128,10240]{1,0:T(8,128)(2,1)}, bf16[128,8192]{1,0:T(8,128)(2,1)}, bf16[128,128]{1,0:T(8,128)(2,1)}, f32[5,2560]{1,0:T(8,128)}, f32[1,2048]{1,0:T(1,128)}, /*index=5*/f32[3,32]{1,0:T(4,128)}) custom-call(bf16[128,10240]{1,0:T(8,128)(2,1)} %bitcast.9, f32[5,2560]{1,0:T(8,128)} %own_conv.1, f32[1,2048]{1,0:T(1,128)} %bitcast.16, ...), custom_call_target="tpu_custom_call" | custom-call | flops 4294967296 | bytes 16777216 | tf_op jit(solution)/shard_map/mixer/pallas_call | solution.py:703
  177.2 5.1 %hand_over.1 = (bf16[128,10240]{1,0:T(8,128)(2,1)}, bf16[128,8192]{1,0:T(8,128)(2,1)}, bf16[128,128]{1,0:T(8,128)(2,1)}, f32[5,2560]{1,0:T(8,128)}, f32[1,2048]{1,0:T(1,128)}, /*index=5*/f32[3,32]{1,0:T(4,128)}) custom-call(bf16[128,10240]{1,0:T(8,128)(2,1)} %get-tuple-element.18.refs_0_, bf16[128,8192]{1,0:T(8,128)(2,1)} %get-tuple-element.19.refs_1_, ...), custom_call_target="tpu_custom_call" | custom-call | tf_op jit(solution)/shard_map/hand_over/pallas_call | solution.py:781
